TPU v7x, 256 devices: a whole 4x4x8 slice. The times are simulated.
256 devices in a mesh: section: 4 (over y), dp: 64 (over z, x, core).
Axes of the slice: x: 4, y: 4, z: 8, core: 2. Of those that a mesh axis runs over, the one named last changes fastest.
Arguments:
- layer_inputs: bfloat16 [4, 8192, 8192], P('section', 'dp'), may hold values from -6 to 6
- top_grad: bfloat16 [8192, 8192], P('dp'), may hold values from -6 to 6
- tenant_ids: int32 [8192], P('dp'), may hold values from 0 to 7
- owner_map: int32 [8], replicated, may hold values from 0 to 63, as said below
- frozen: bfloat16 [4, 8192, 1024], P('section', 'dp'), may hold values from -0.0625 to 0.0625
- adapt_a: bfloat16 [4, 8192, 128], P('section', 'dp'), may hold values from -0.0625 to 0.0625
- adapt_b: bfloat16 [4, 128, 512], P('section'), may hold values from -0.25 to 0.25
Outputs:
- grads_in: bfloat16 [4, 8192, 8192], P('section', 'dp')
- owned_a: float32 [4, 64, 16, 8192], P('section', 'dp')
- owned_b: float32 [4, 64, 16, 512], P('section', 'dp')
Inputs may be any that keep to these rules, and one draw needn't show every extreme that they name: `owner_map`: distinct owners for distinct tenants.
All inputs are finite; a program needn't handle non-finite values.
Results may differ from a plain program's by a relative error of at most 0.011.
Values may be sent and summed in bfloat16 or wider, within the bound.
A program may use at most 192 MiB of HBM per device.

v0:
```python
import jax
import jax.numpy as jnp
from jax import lax
from jax.sharding import PartitionSpec as P


def from_behind(x, axis, by):
    count = lax.axis_size(axis)
    pairs = [(i, i + by) for i in range(count) if 0 <= i + by < count]
    return lax.ppermute(x, axis, pairs)


def body(layer_inputs, top_grad, tenant_ids, owner_map, frozen, adapt_a, adapt_b):
    scale = 2.0
    sections = lax.axis_size("section")
    my_section = lax.axis_index("section")
    my_data = lax.axis_index("dp")
    inputs = layer_inputs[0]
    upmap = adapt_b[0]
    full_frozen, down = (
        lax.all_gather(frozen[0], "dp", axis=0, tiled=True),
        lax.all_gather(adapt_a[0], "dp", axis=0, tiled=True),
    )
    kv_width = upmap.shape[1]
    total_cols = upmap.shape[0]
    rank_size = total_cols // owner_map.shape[0]
    tenant_count = owner_map.shape[0]
    width = down.shape[0]
    w_value = full_frozen[:, :kv_width]
    out_t = full_frozen[:, kv_width:]
    columns = lax.broadcasted_iota(jnp.int32, (1, total_cols), 1) // rank_size

    def chain_layer(grad, ids):
        mask = (columns == ids[:, None]).astype(jnp.float32)
        value_grad = jnp.dot(grad, out_t, preferred_element_type=jnp.float32).astype(jnp.bfloat16)
        back = (
            mask
            * lax.dot_general(
                value_grad, upmap, (((1,), (1,)), ((), ())), preferred_element_type=jnp.float32
            )
        ).astype(jnp.bfloat16)
        total = grad.astype(jnp.float32) + lax.dot_general(
            value_grad, w_value, (((1,), (1,)), ((), ())), preferred_element_type=jnp.float32
        )
        total = total + scale * lax.dot_general(
            back, down, (((1,), (1,)), ((), ())), preferred_element_type=jnp.float32
        )
        return (total.astype(jnp.bfloat16), value_grad)

    def skipped(grad, ids):
        return (
            jnp.zeros(grad.shape, jnp.bfloat16),
            jnp.zeros((grad.shape[0], kv_width), jnp.bfloat16),
        )

    rows = inputs.shape[0]
    grads = jnp.zeros((rows, width), jnp.bfloat16)
    values = jnp.zeros((rows, kv_width), jnp.bfloat16)
    grad = top_grad
    for step in range(sections):
        active = my_section == sections - 1 - step
        grad_in, value_grad = lax.cond(active, chain_layer, skipped, grad, tenant_ids)
        grads = jnp.where(active, grad_in, grads)
        values = jnp.where(active, value_grad, values)
        if step < sections - 1:
            grad = from_behind(grad_in, "section", -1)
    mask = (columns == tenant_ids[:, None]).astype(jnp.float32)
    low = (mask * jnp.dot(inputs, down, preferred_element_type=jnp.float32)).astype(jnp.bfloat16)
    back = (
        mask
        * lax.dot_general(
            values, upmap, (((1,), (1,)), ((), ())), preferred_element_type=jnp.float32
        )
    ).astype(jnp.bfloat16)
    sum_a = scale * lax.dot_general(
        inputs, back, (((0,), (0,)), ((), ())), preferred_element_type=jnp.float32
    )
    sum_b = scale * lax.dot_general(
        low, values, (((0,), (0,)), ((), ())), preferred_element_type=jnp.float32
    )
    full_a, full_b = lax.psum((sum_a, sum_b), "dp")
    owned = (owner_map == my_data).astype(jnp.float32)
    owned_a = jnp.einsum(
        "dtr,t->rd",
        full_a.reshape(width, tenant_count, rank_size),
        owned,
        precision=lax.Precision.HIGHEST,
    )
    owned_b = jnp.einsum(
        "trk,t->rk",
        full_b.reshape(tenant_count, rank_size, kv_width),
        owned,
        precision=lax.Precision.HIGHEST,
    )
    owned_a = owned_a[None, None]
    owned_b = owned_b[None, None]
    return (grads[None], owned_a, owned_b)


def solution(mesh):
    return jax.shard_map(
        body,
        mesh=mesh,
        in_specs=(
            P("section", "dp", None),
            P("dp", None),
            P("dp"),
            P(),
            P("section", "dp", None),
            P("section", "dp", None),
            P("section", None, None),
        ),
        out_specs=(
            P("section", "dp", None),
            P("section", "dp", None, None),
            P("section", "dp", None, None),
        ),
        check_vma=False,
    )
```

profile of v0, /device:TPU:1, one launch (start us, length us, event | category | flops | bytes accessed | tf_op | source)
XLA Modules:
  0.0 709.6 jit_solution(6698406435156345612)
XLA Ops:
  8.7 106.0 %all-gather.5.cloned.1.call-done = bf16[1,8192,1024]{2,1,0:T(8,128)(2,1)} async-done(((bf16[1,128,1024]{2,1,0:T(8,128)(2,1)}), bf16[1,8192,1024]{2,1,0:T(8,128)(2,1)}) %all-gather.5.cloned.1.call-update) | async-done | bytes 16777232 | tf_op jit(solution)/shard_map/all_gather | solution.py:21
  114.7 11.4 %fusion.68 = (bf16[8192,512]{1,0:T(8,128)(2,1)}, bf16[8192,512]{1,0:T(8,128)(2,1)}) fusion(bf16[8192,1024]{1,0:T(8,128)(2,1)} %bitcast.82), kind=kLoop, calls=%fused_computation.90 | loop fusion | bytes 33554432 | tf_op jit(solution)/shard_map/slice | solution.py:29
  126.1 65.6 %all-gather.7.cloned.1.call-done = bf16[1,8192,128]{2,1,0:T(8,128)(2,1)} async-done(((bf16[1,128,128]{2,1,0:T(8,128)(2,1)}), bf16[1,8192,128]{2,1,0:T(8,128)(2,1)}) %all-gather.7.cloned.1.call-update) | async-done | bytes 2097168 | tf_op jit(solution)/shard_map/all_gather | solution.py:22
  191.7 2.2 conditional.4
  192.4 1.5 broadcast.104
  193.9 1.3 collective-permute-start
  195.2 47.9 %collective-permute-done = bf16[128,8192]{1,0:T(8,128)(2,1)} collective-permute-done((bf16[128,8192]{1,0:T(8,128)(2,1)}, bf16[128,8192]{1,0:T(8,128)(2,1)}, u32[]{:S(2)}, u32[]{:S(2)}) %collective-permute-start) | collective-permute-done | bytes 2097184 | tf_op jit(solution)/shard_map/ppermute | solution.py:10
  243.1 2.3 conditional.5
  243.8 1.6 broadcast.108
  246.7 47.0 %collective-permute-done.1 = bf16[128,8192]{1,0:T(8,128)(2,1)} collective-permute-done((bf16[128,8192]{1,0:T(8,128)(2,1)}, bf16[128,8192]{1,0:T(8,128)(2,1)}, u32[]{:S(2)}, u32[]{:S(2)}) %collective-permute-start.1) | collective-permute-done | bytes 2097184 | tf_op jit(solution)/shard_map/ppermute | solution.py:10
  293.7 2.3 conditional.6
  294.3 1.6 broadcast.112
  297.2 93.4 %collective-permute-done.2 = bf16[128,8192]{1,0:T(8,128)(2,1)} collective-permute-done((bf16[128,8192]{1,0:T(8,128)(2,1)}, bf16[128,8192]{1,0:T(8,128)(2,1)}, u32[]{:S(2)}, u32[]{:S(2)}) %collective-permute-start.2) | collective-permute-done | bytes 2097184 | tf_op jit(solution)/shard_map/ppermute | solution.py:10
  390.6 18.0 %conditional.7 = (bf16[128,8192]{1,0:T(8,128)(2,1)}, bf16[128,512]{1,0:T(8,128)(2,1)}) conditional(s32[]{:T(128)} %convert_element_type.72, () %tuple.40, (bf16[128,8192]{1,0:T(8,128)(2,1)}, bf16[8192,512]{1,0:T(8,128)(2,1)}, bf16[8192,512]{1,0:T(8,128)(2,1)}, s32[1,128]{1,0:T(1,128)S(1)}, s32[128]{0:T(128)S(1)}, ...), branch_computations={%region_6.7_spmd, %region_7.8_spmd} | conditional | flops 2438053888 | bytes 67634224 | solution.py:62
  390.6 6.1 convolution_convert_fusion.3
  397.0 6.5 convolution_add_fusion.3
  403.5 5.1 fusion.25
  409.6 2.9 convolution_multiply_fusion.4
  412.5 3.2 convolution_multiply_fusion.5
  415.7 3.3 select_bitcast_fusion
  419.0 188.2 %all-reduce.3.cloned.1.call-done = (f32[8192,8,16]{0,2,1:T(8,128)}, f32[8,16,512]{2,1,0:T(8,128)}) async-done(((f32[8192,8,16]{0,2,1:T(8,128)}, f32[8,16,512]{2,1,0:T(8,128)}), (f32[8192,8,16]{0,2,1:T(8,128)}, f32[8,16,512]{2,1,0:T(8,128)})) %all-reduce.3.cloned.1.call-update) | async-done | bytes 4456464 | tf_op jit(solution)/shard_map/psum | solution.py:81
  607.2 1.3 fusion.46
  609.2 58.0 %fusion.32 = f32[1,8192,16]{0,1,2:T(8,128)} fusion(f32[8192,8,16]{0,2,1:T(8,128)} %get-tuple-element.105, s32[8]{0:T(128)S(1)} %copy-done.9, s32[]{:T(128)S(6)} %axis_index.25), kind=kOutput, calls=%fused_computation.49 | convolution fusion | flops 12582920 | bytes 4718628 | tf_op jit(solution)/shard_map/dtr,t->rd/dot_general | solution.py:83
  667.2 35.9 %copy.12 = f32[1,8192,16]{1,2,0:T(8,128)} copy(f32[1,8192,16]{0,1,2:T(8,128)} %fusion.32) | data formatting | bytes 1048576 | tf_op jit(solution)/shard_map/dtr,t->rd/dot_general | solution.py:83
  (27 shorter events, 8.0 us)
Async XLA Ops:
  7.2 402.4 %copy-start = (bf16[1,128,8192]{2,1,0:T(8,128)(2,1)S(1)}, bf16[1,128,8192]{2,1,0:T(8,128)(2,1)}, u32[]{:S(2)}) copy-start(bf16[1,128,8192]{2,1,0:T(8,128)(2,1)} %param.15) | copy-start | bytes 6291460
  7.2 107.6 %all-gather.5.cloned.1.call-start = ((), (), s32[]{:S(2)}) async-start(), calls=%async_computation | async-start | bytes 17039360 | tf_op jit(solution)/shard_map/all_gather | solution.py:21
  7.9 183.8 %all-gather.7.cloned.1.call-start = ((), (), s32[]{:S(2)}) async-start(), calls=%async_computation.1 | async-start | bytes 2129920 | tf_op jit(solution)/shard_map/all_gather | solution.py:22
  8.7 598.6 %all-reduce.3.cloned.1.call-start = ((), (), s32[]{:S(2)}) async-start(), calls=%async_computation.2 | async-start | bytes 8912896 | tf_op jit(solution)/shard_map/psum | solution.py:81
  114.7 77.0 %copy-start.7 = (bf16[1,128,512]{2,1,0:T(8,128)(2,1)S(1)}, bf16[1,128,512]{2,1,0:T(8,128)(2,1)}, u32[]{:S(2)}) copy-start(bf16[1,128,512]{2,1,0:T(8,128)(2,1)} %param.21) | copy-start | bytes 393220
  114.7 77.0 %copy-start.8 = (s32[128]{0:T(128)S(1)}, s32[128]{0:T(128)}, u32[]{:S(2)}) copy-start(s32[128]{0:T(128)} %param.17) | copy-start | bytes 1540
  193.9 49.2 %collective-permute-start = (bf16[128,8192]{1,0:T(8,128)(2,1)}, bf16[128,8192]{1,0:T(8,128)(2,1)}, u32[]{:S(2)}, u32[]{:S(2)}) collective-permute-start(bf16[128,8192]{1,0:T(8,128)(2,1)} %get-tuple-element.95), channel_id=1, source_target_pairs={{64,0},{128,64},{192,128},{65,1},{129,65},{193,129},{66,2},{130,66... | collective-permute-start | bytes 6291464 | tf_op jit(solution)/shard_map/ppermute | solution.py:10
  245.4 48.3 %collective-permute-start.1 = (bf16[128,8192]{1,0:T(8,128)(2,1)}, bf16[128,8192]{1,0:T(8,128)(2,1)}, u32[]{:S(2)}, u32[]{:S(2)}) collective-permute-start(bf16[128,8192]{1,0:T(8,128)(2,1)} %get-tuple-element.96), channel_id=1, source_target_pairs={{64,0},{128,64},{192,128},{65,1},{129,65},{193,129},{66,2},{130,66... | collective-permute-start | bytes 6291464 | tf_op jit(solution)/shard_map/ppermute | solution.py:10
  295.9 94.7 %collective-permute-start.2 = (bf16[128,8192]{1,0:T(8,128)(2,1)}, bf16[128,8192]{1,0:T(8,128)(2,1)}, u32[]{:S(2)}, u32[]{:S(2)}) collective-permute-start(bf16[128,8192]{1,0:T(8,128)(2,1)} %get-tuple-element.97), channel_id=1, source_target_pairs={{64,0},{128,64},{192,128},{65,1},{129,65},{193,129},{66,2},{130,66... | collective-permute-start | bytes 6291464 | tf_op jit(solution)/shard_map/ppermute | solution.py:10
  390.6 6.4 copy-start.5
  415.7 191.5 %copy-start.9 = (s32[8]{0:T(128)S(1)}, s32[8]{0:T(128)}, u32[]{:S(2)}) copy-start(s32[8]{0:T(128)} %param.18) | copy-start | bytes 100
  667.2 35.9 %copy-start.1 = (bf16[1,128,8192]{2,1,0:T(8,128)(2,1)S(1)}, bf16[1,128,8192]{2,1,0:T(8,128)(2,1)}, u32[]{:S(2)}) copy-start(bf16[1,128,8192]{2,1,0:T(8,128)(2,1)} %param.15) | copy-start | bytes 6291460
Sparse Core Ops, SparseCore 0:
  10.8 103.9 all-gather.4
  117.5 74.1 all-gather.6
  415.8 191.3 all-reduce.2
where the time goes:
time: 711 us; the launch traced here: 710 us
  waiting for transfers between devices  550 us (77%)
  matrix products  83.1 us (12%)
  local copies, waits for them, and re-layouts  54.9 us (8%)
  between operations  13.8 us (2%)
    ppermute x3, waiting for transfers between devices, from_behind(): return lax.ppermute(x, axis, pairs)  188 us
    psum x1, waiting for transfers between devices, body(): full_a, full_b = lax.psum((sum_a, sum_b), 'dp')  188 us
    all_gather x1, waiting for transfers between devices, body(): lax.all_gather(frozen[0], 'dp', axis=0, tiled=True)  106 us
    all_gather x1, waiting for transfers between devices, body(): lax.all_gather(adapt_a[0], 'dp', axis=0, tiled=True)  65.6 us
    dot_general x1, matrix products, body(): jnp.einsum('dtr,t->rd', full_a.reshape(width, tenant_count, rank_size), o...  58 us
    dot_general x1, local copies, waits for them, and re-layouts, body(): jnp.einsum('dtr,t->rd', full_a.reshape(width, tenant_count, rank_size), o...  35.9 us
  transfers between devices with their start and end apart: 6, of which 6 were waited for; matrix products, arithmetic and copies ran while one was open for 2% of the time, Pallas kernels for 0%

commit v1 on v0

v1 whole, which is shorter than its diff:
```python
import functools

import jax
import jax.numpy as jnp
from jax import lax
from jax.experimental import pallas as pl
from jax.experimental.pallas import tpu as pltpu
from jax.sharding import PartitionSpec as P

MESH = pl.DeviceIdType.MESH
NY, NZ, NX, NC = 4, 8, 4, 2
D = 8192
KV = 512
TR = 128
RANK = 16
WA = KV + TR
ROWS = 128
SUB = ROWS // NY
COLS = NZ * NX * SUB


def mm(a, b):
    return lax.dot_general(a, b, (((1,), (0,)), ((), ())), preferred_element_type=jnp.float32)


def mm_t(a, b):
    return lax.dot_general(a, b, (((1,), (1,)), ((), ())), preferred_element_type=jnp.float32)


def chain_kernel(
    g0_ref, fz_ref, aa_ref, bb_ref, ids_ref,
    out_ref, vb_ref,
    ob, wab, gall, rbuf, g0v, gsend, pb, rsr, vball, bbuf, perm,
    ring_s, ring_r, y_s, yo_r, yw_r, b_r, g_sem, sib_sem, rs_s, rs_r, vb_s, vb_r, out_s, out_r,
):
    y = lax.axis_index("section")
    d = lax.axis_index("dp")
    z = d // (NX * NC)
    x = (d // NC) % NX
    c = d % NC

    def dev(yy, zz, xx, cc):
        return (yy, zz * (NX * NC) + xx * NC + cc)

    xr, xl = (x + 1) % NX, (x + NX - 1) % NX
    xo = (x + 2) % NX
    zr, zl = (z + 1) % NZ, (z + NZ - 1) % NZ
    sib = 1 - c
    pending = []

    def send(src, dst, ssem, rsem, device):
        copy = pltpu.make_async_remote_copy(
            src_ref=src, dst_ref=dst, send_sem=ssem, recv_sem=rsem,
            device_id=device, device_id_type=MESH,
        )
        copy.start()
        pending.append(copy)

    def landed(dst, rsem):
        pltpu.make_async_copy(dst, dst, rsem).wait()

    load = pltpu.make_async_copy(g0_ref, g0v, g_sem)
    load.start()

    column = [
        (dq, dc, (y + dq) % NY, (c + dc) % NC)
        for dq in range(NY) for dc in range(NC) if dq or dc
    ]
    barrier = pltpu.get_barrier_semaphore()
    for _, _, yy, cc in column:
        pl.semaphore_signal(barrier, inc=1, device_id=dev(yy, z, x, cc), device_id_type=MESH)
    for zz, xx in ((z, xr), (z, xl), (zr, x), (zl, x)):
        pl.semaphore_signal(barrier, inc=1, device_id=dev(y, zz, xx, c), device_id_type=MESH)
    pl.semaphore_wait(barrier, 11)

    local = []
    for dq in range(NY):
        yy = (y + dq) % NY
        rows = pl.ds(pl.multiple_of(yy * SUB, SUB), SUB)
        parts = (
            (fz_ref.at[rows, pl.ds(KV, KV)], ob.at[y, z, x], yo_r.at[y]),
            (fz_ref.at[rows, pl.ds(0, KV)], wab.at[y, z, x, :, pl.ds(0, KV)], yw_r.at[y]),
            (aa_ref.at[rows, :], wab.at[y, z, x, :, pl.ds(KV, TR)], yw_r.at[y]),
            (bb_ref, bbuf.at[y], b_r.at[y]),
        )
        for i, (src, dst, rsem) in enumerate(parts):
            if dq:
                send(src, dst, y_s.at[dq, i], rsem, dev(yy, z, x, c))
            else:
                copy = pltpu.make_async_copy(src, dst, rsem)
                copy.start()

    half = SUB // 2

    def ring(piece, k):
        s = NY - 1 - piece // 2
        is_o = piece % 2 == 0
        buf = ob if is_o else wab
        width = KV if is_o else WA
        lo, hi = pl.ds(0, 256), pl.ds(256, width - 256)
        top, low = pl.ds(0, half), pl.ds(half, half)

        def step(part, stage, moves):
            for way, (src, dst) in enumerate(moves):
                zz, xx = dst
                send(src, src, ring_s.at[piece, part, stage, way],
                     ring_r.at[piece, part, stage, way], dev(y, zz, xx, c))

        def arrive(part, stage, refs):
            for way, ref in enumerate(refs):
                landed(ref, ring_r.at[piece, part, stage, way])

        def zb(by):
            return (z + by + NZ) % NZ

        right, left = (z, xr), (z, xl)
        up, down = (zr, x), (zl, x)
        a_recv = [
            (buf.at[s, z, xl, top], buf.at[s, z, xr, top]),
            (buf.at[s, z, xo, top, lo], buf.at[s, z, xo, top, hi]),
            (buf.at[s, zb(-1), :, top], buf.at[s, zb(1), :, top]),
            (buf.at[s, zb(-2), :, top], buf.at[s, zb(2), :, top]),
            (buf.at[s, zb(-3), :, top], buf.at[s, zb(3), :, top]),
            (buf.at[s, zb(4), pl.ds(0, 2), top], buf.at[s, zb(4), pl.ds(2, 2), top]),
        ]
        a_send = [
            ((buf.at[s, z, x, top], right), (buf.at[s, z, x, top], left)),
            ((buf.at[s, z, xl, top, lo], right), (buf.at[s, z, xr, top, hi], left)),
            ((buf.at[s, z, :, top], up), (buf.at[s, z, :, top], down)),
            ((buf.at[s, zb(-1), :, top], up), (buf.at[s, zb(1), :, top], down)),
            ((buf.at[s, zb(-2), :, top], up), (buf.at[s, zb(2), :, top], down)),
            ((buf.at[s, zb(-3), pl.ds(0, 2), top], up), (buf.at[s, zb(3), pl.ds(2, 2), top], down)),
        ]
        b_recv = [
            (buf.at[s, zb(-1), x, low], buf.at[s, zb(1), x, low]),
            (buf.at[s, zb(-2), x, low], buf.at[s, zb(2), x, low]),
            (buf.at[s, zb(-3), x, low], buf.at[s, zb(3), x, low]),
            (buf.at[s, zb(4), x, low, lo], buf.at[s, zb(4), x, low, hi]),
            (buf.at[s, :, xl, low], buf.at[s, :, xr, low]),
            (buf.at[s, pl.ds(0, 4), xo, low], buf.at[s, pl.ds(4, 4), xo, low]),
        ]
        b_send = [
            ((buf.at[s, z, x, low], up), (buf.at[s, z, x, low], down)),
            ((buf.at[s, zb(-1), x, low], up), (buf.at[s, zb(1), x, low], down)),
            ((buf.at[s, zb(-2), x, low], up), (buf.at[s, zb(2), x, low], down)),
            ((buf.at[s, zb(-3), x, low, lo], up), (buf.at[s, zb(3), x, low, hi], down)),
            ((buf.at[s, :, x, low], right), (buf.at[s, :, x, low], left)),
            ((buf.at[s, pl.ds(0, 4), xl, low], right), (buf.at[s, pl.ds(4, 4), xr, low], left)),
        ]
        if k == 0:
            landed(buf.at[s, z, x], (yo_r if is_o else yw_r).at[s])
        else:
            arrive(0, k - 1, a_recv[k - 1])
            arrive(1, k - 1, b_recv[k - 1])
        if k < 6:
            step(0, k, a_send[k])
            step(1, k, b_send[k])

    def compact():
        load.wait()
        source = lax.broadcasted_iota(jnp.int32, (NX * NC * ROWS, ROWS), 0)
        target = lax.broadcasted_iota(jnp.int32, (NX * NC * ROWS, ROWS), 1)
        base = (target // SUB) * (NC * ROWS) + target % SUB + y * SUB
        mine = (source == base + c * ROWS).astype(jnp.bfloat16)
        other = (source == base + sib * ROWS).astype(jnp.bfloat16)
        own = pl.ds(pl.multiple_of(c * ROWS, ROWS), ROWS)

        for zz in range(NZ):
            block = g0v[:, zz * 1024:(zz + 1) * 1024]
            gsend[:, zz * ROWS:(zz + 1) * ROWS] = mm(block, other).astype(jnp.bfloat16)
        send(gsend, gall.at[NY, own], sib_sem.at[0], sib_sem.at[1], dev(y, z, x, sib))
        for zz in range(NZ):
            block = g0v[:, zz * 1024:(zz + 1) * 1024]
            gall[NY, own, zz * ROWS:(zz + 1) * ROWS] = mm(block, mine).astype(jnp.bfloat16)
        landed(gsend, sib_sem.at[1])

        p_in = lax.broadcasted_iota(jnp.int32, (NY * ROWS, NY * ROWS), 0)
        p_out = lax.broadcasted_iota(jnp.int32, (NY * ROWS, NY * ROWS), 1)
        want = ((p_out // SUB) % NY) * ROWS + (p_out // ROWS) * SUB + p_out % SUB
        perm[...] = (p_in == want).astype(jnp.bfloat16)

    def block_of(yy, cc):
        return pl.ds(pl.multiple_of(cc * ROWS + yy * SUB, SUB), SUB)

    def partial(s):
        right = ob[s].reshape(COLS, KV)
        pb[s] = mm(gall[s + 1], right).astype(jnp.bfloat16)
        for dq, dc, yy, cc in column:
            j = dq * NC + dc
            send(pb.at[s, block_of(yy, cc)], rsr.at[s, j], rs_s.at[s, j], rs_r.at[s, j], dev(yy, z, x, cc))

    def finalise(s):
        total = pb[s, block_of(y, c), :].astype(jnp.float32)
        for dq, dc, _, _ in column:
            j = dq * NC + dc
            landed(rsr.at[s, j], rs_r.at[s, j])
            total = total + rsr[s, j].astype(jnp.float32)
        value = total.astype(jnp.bfloat16)
        landed(bbuf.at[s], b_r.at[s])
        ids = ids_ref[pl.ds(pl.multiple_of(y * SUB, SUB), SUB), :]
        columns = lax.broadcasted_iota(jnp.int32, (SUB, TR), 1) // RANK
        mask = (columns == ids).astype(jnp.float32)
        back = (mask * mm_t(value, bbuf[s])).astype(jnp.bfloat16)
        here = block_of(y, c)
        vball[s, here, 0:KV] = value
        vball[s, here, KV:WA] = (2.0 * back.astype(jnp.float32)).astype(jnp.bfloat16)
        for dq, dc, yy, cc in column:
            j = dq * NC + dc
            send(vball.at[s, here], vball.at[s, here], vb_s.at[s, j], vb_r.at[s, j], dev(yy, z, x, cc))

    def update(s):
        for dq, dc, _, _ in column:
            j = dq * NC + dc
            there = block_of((y - dq + NY) % NY, (c - dc + NC) % NC)
            landed(vball.at[s, there], vb_r.at[s, j])
        for i in range(4):
            cols = slice(i * 256, (i + 1) * 256)
            right = wab[s, 2 * i:2 * i + 2].reshape(256, WA)
            delta = mm_t(vball[s], right)
            gall[s, :, cols] = (gall[s + 1, :, cols].astype(jnp.float32) + delta).astype(jnp.bfloat16)
        own = pl.ds(pl.multiple_of(c * ROWS, ROWS), ROWS)
        others = pl.ds(pl.multiple_of(sib * ROWS, ROWS), ROWS)
        dq = (s - y + NY) % NY
        send(gall.at[s, others], rbuf.at[y, c], out_s.at[s, 1], out_r.at[dq * 2 + 1], dev(s, z, x, sib))
        direct = pltpu.make_async_remote_copy(
            src_ref=gall.at[s, own], dst_ref=rbuf.at[y, c], send_sem=out_s.at[s, 0], recv_sem=out_r.at[dq * 2],
            device_id=dev(s, z, x, c), device_id_type=MESH,
        )
        keep = pltpu.make_async_copy(gall.at[s, own], rbuf.at[y, c], out_r.at[0])

        @pl.when(y != s)
        def _():
            direct.start()

        @pl.when(y == s)
        def _():
            keep.start()

    compact()
    for t in range(15):
        for piece in range(8):
            if 0 <= t - piece <= 6:
                ring(piece, t - piece)
        if t >= 6 and t % 2 == 0:
            i = (t - 6) // 2
            if i > 0:
                update(NY - i)
            if i < NY:
                partial(NY - 1 - i)
        elif t >= 7:
            finalise(NY - 1 - (t - 7) // 2)

    vb_ref[...] = vball[y, pl.ds(pl.multiple_of(c * ROWS, ROWS), ROWS), :]
    for j in range(NY * NC):
        landed(rbuf.at[(y - j // 2 + NY) % NY, (c - j % 2 + NC) % NC], out_r.at[j])
    for zz in range(NZ):
        for cc in range(NC):
            block = jnp.concatenate([rbuf[q, cc, :, zz * ROWS:(zz + 1) * ROWS] for q in range(NY)], axis=1)
            mixed = mm(block, perm[...]).astype(jnp.bfloat16)
            for xx in range(NX):
                at = zz * 1024 + xx * 256 + cc * ROWS
                out_ref[:, at:at + ROWS] = mixed[:, xx * ROWS:(xx + 1) * ROWS]

    for s in range(NY):
        @pl.when(y != s)
        def _(s=s):
            own = pl.ds(pl.multiple_of(c * ROWS, ROWS), ROWS)
            pltpu.make_async_copy(gall.at[s, own], gall.at[s, own], out_s.at[s, 0]).wait()
    for copy in pending:
        copy.wait_send()


def chain(g0, fz, aa, bb, ids):
    vmem = pl.BlockSpec(memory_space=pltpu.VMEM)
    dma = pltpu.SemaphoreType.DMA
    bf = jnp.bfloat16
    return pl.pallas_call(
        chain_kernel,
        out_shape=(
            jax.ShapeDtypeStruct((ROWS, D), bf),
            jax.ShapeDtypeStruct((ROWS, WA), bf),
        ),
        in_specs=[pl.BlockSpec(memory_space=pl.ANY), vmem, vmem, vmem, vmem],
        out_specs=(vmem, vmem),
        scratch_shapes=[
            pltpu.VMEM((NY, NZ, NX, SUB, KV), bf),
            pltpu.VMEM((NY, NZ, NX, SUB, WA), bf),
            pltpu.VMEM((NY + 1, NC * ROWS, COLS), bf),
            pltpu.VMEM((NY, NC, ROWS, COLS), bf),
            pltpu.VMEM((ROWS, D), bf),
            pltpu.VMEM((ROWS, COLS), bf),
            pltpu.VMEM((NY, NC * ROWS, KV), bf),
            pltpu.VMEM((NY, NY * NC, SUB, KV), bf),
            pltpu.VMEM((NY, NC * ROWS, WA), bf),
            pltpu.VMEM((NY, TR, KV), bf),
            pltpu.VMEM((NY * ROWS, NY * ROWS), bf),
            dma((8, 2, 6, 2)),
            dma((8, 2, 6, 2)),
            dma((NY, 4)),
            dma((NY,)),
            dma((NY,)),
            dma((NY,)),
            dma,
            dma((2,)),
            dma((NY, NY * NC)),
            dma((NY, NY * NC)),
            dma((NY, NY * NC)),
            dma((NY, NY * NC)),
            dma((NY, 2)),
            dma((NY * NC,)),
        ],
        compiler_params=pltpu.CompilerParams(
            collective_id=0, has_side_effects=True, vmem_limit_bytes=50 * 2**20
        ),
        cost_estimate=pl.CostEstimate(flops=4 * 10**9, bytes_accessed=10**7, transcendentals=0),
    )(g0, fz, aa, bb, ids)


def body(layer_inputs, top_grad, tenant_ids, owner_map, frozen, adapt_a, adapt_b):
    my_data = lax.axis_index("dp")
    inputs = layer_inputs[0]
    down = lax.all_gather(adapt_a[0], "dp", axis=0, tiled=True)
    grads, vb = chain(top_grad, frozen[0], adapt_a[0], adapt_b[0], tenant_ids[:, None])
    values, back2 = vb[:, :KV], vb[:, KV:]
    columns = lax.broadcasted_iota(jnp.int32, (1, TR), 1) // RANK
    mask = (columns == tenant_ids[:, None]).astype(jnp.float32)
    low = (mask * mm(inputs, down)).astype(jnp.bfloat16)
    sum_a = lax.dot_general(back2, inputs, (((0,), (0,)), ((), ())), preferred_element_type=jnp.float32)
    sum_b = 2.0 * lax.dot_general(low, values, (((0,), (0,)), ((), ())), preferred_element_type=jnp.float32)
    full = lax.psum(jnp.concatenate([sum_a, sum_b], axis=1), "dp")
    owned = (owner_map == my_data).astype(jnp.float32)
    mine = jnp.sum(full.reshape(-1, RANK, D + KV) * owned[:, None, None], axis=0)
    return grads[None], mine[None, None, :, :D], mine[None, None, :, D:]


def solution(mesh):
    return jax.shard_map(
        body,
        mesh=mesh,
        in_specs=(
            P("section", "dp", None),
            P("dp", None),
            P("dp"),
            P(),
            P("section", "dp", None),
            P("section", "dp", None),
            P("section", None, None),
        ),
        out_specs=(
            P("section", "dp", None),
            P("section", "dp", None, None),
            P("section", "dp", None, None),
        ),
        check_vma=False,
    )
```

time: 711 us -> 420 us (0.59)
  waiting for transfers between devices: 550 us -> 190 us
  Pallas kernels: 0 us -> 194 us
  matrix products: 83.1 us -> 5.22 us
  local copies, waits for them, and re-layouts: 54.9 us -> 8.09 us
    pallas_call x0 -> x1, Pallas kernels: none -> 194 us  [chain(): pl.pallas_call(chain_kernel, out_shape=(jax.ShapeDtypeStruct((ROWS, D), b...]
    ppermute x3 -> x0, waiting for transfers between devices: 188 us -> none  [from_behind(): return lax.ppermute(x, axis, pairs)]
    all_gather x2 -> x1, waiting for transfers between devices: 172 us -> 0.01 us  [body(): down = lax.all_gather(adapt_a[0], 'dp', axis=0, tiled=True)]
    dot_general x6 -> x1, matrix products: 79.9 us -> 2.74 us  [body(): lax.dot_general(back2, inputs, (((0,), (0,)), ((), ())), preferred_elemen...]
    dot_general x2 -> x0, local copies, waits for them, and re-layouts: 36.5 us -> none  [the longest x1 35.9 us: body(): jnp.einsum('dtr,t->rd', full_a.reshape(width, tenant_count, rank_size), o...]
    slice x1 -> x0, local copies, waits for them, and re-layouts: 11.4 us -> none  [body(): w_value = full_frozen[:, :kv_width]]
  transfers between devices with their start and end apart: 6 -> 2, of which waited for: 6 -> 1; matrix products, arithmetic and copies ran while one was open for 2% -> 1% of each run, Pallas kernels for 0% -> 46%
where the time goes in v1:
time: 420 us; the launch traced here: 419 us
  Pallas kernels  194 us (46%)
  waiting for transfers between devices  190 us (45%)
  between operations  14.1 us (3%)
  local copies, waits for them, and re-layouts  8.09 us (2%)
  other arithmetic  7.48 us (2%)
  matrix products  5.22 us (1%)
    pallas_call x1, Pallas kernels, chain(): pl.pallas_call(chain_kernel, out_shape=(jax.ShapeDtypeStruct((ROWS, D), b...  194 us
    psum x1, waiting for transfers between devices, body(): full = lax.psum(jnp.concatenate([sum_a, sum_b], axis=1), 'dp')  189 us
  transfers between devices with their start and end apart: 2, of which 1 were waited for; matrix products, arithmetic and copies ran while one was open for 1% of the time, Pallas kernels for 46%

profile of v1, /device:TPU:1, one launch (start us, length us, event | category | flops | bytes accessed | tf_op | source)
XLA Modules:
  0.0 418.8 jit_solution(15688781111155712714)
XLA Ops:
  7.2 0.0 copy-start
  7.2 0.0 all-gather.3.cloned.1.call-start
  7.2 0.7 all-gather.3.cloned.1.call-update
  7.9 0.0 all-reduce.2.cloned.1.call-start
  8.0 0.8 copy.10.ids_ref
  8.7 0.0 copy-start.3
  8.7 0.7 copy-done.3
  9.5 0.9 copy-done.4
  10.4 0.9 copy-done.5
  11.3 193.8 %shard_map.94 = (bf16[128,8192]{1,0:T(8,128)(2,1)S(1)}, bf16[128,640]{1,0:T(8,128)(2,1)S(1)}) custom-call(bf16[128,8192]{1,0:T(8,128)(2,1)} %g0_ref.1, bf16[128,1024]{1,0:T(8,128)(2,1)S(1)} %bitcast.32, bf16[128,128]{1,0:T(8,128)(2,1)S(1)} %bitcast.31, bf16[128,512]{1,0:T(8,128)(2,1)S(1)} %bitcast.33, s32[128,1]{1,0:T(8,128)S(1)} %copy.10.ids_ref), custom_call_target="tpu_custom_call" | custom-call | flops 4000000000 | bytes 10000000 | tf_op jit(solution)/shard_map/pallas_call | solution.py:277
  205.1 0.0 copy-start.1
  205.2 1.3 copy-done.1
  206.5 0.0 copy-done
  206.5 2.7 fusion.3
  209.2 0.0 copy-done.6
  209.2 2.5 convolution_multiply_fusion
  211.7 4.6 %pad_maximum_fusion = f32[128,8704]{1,0:T(8,128)} fusion(f32[128,512]{1,0:T(8,128)S(1)} %convolution_multiply_fusion, f32[128,8192]{1,0:T(8,128)} %fusion.3), kind=kLoop, calls=%fused_computation | loop fusion | flops 1114112 | bytes 8912896 | tf_op jit(solution)/shard_map/concatenate | solution.py:330
  216.3 0.0 all-reduce.2.cloned.1.call-update
  216.3 0.6 copy-done.7
  217.0 189.3 %all-reduce.2.cloned.1.call-done = f32[8,16,8704]{2,1,0:T(8,128)} async-done(((f32[8,16,8704]{2,1,0:T(8,128)}), f32[8,16,8704]{2,1,0:T(8,128)}) %all-reduce.2.cloned.1.call-update) | async-done | bytes 4456464 | tf_op jit(solution)/shard_map/psum | solution.py:330
  406.3 2.9 multiply_reduce_fusion
  409.2 0.8 slice_bitcast_fusion
  410.0 0.6 slice_bitcast_fusion.1
  410.6 1.3 copy.13
  (9 shorter events, 0.0 us)
Async XLA Ops:
  7.2 199.3 %copy-start = (bf16[1,128,8192]{2,1,0:T(8,128)(2,1)S(1)}, bf16[1,128,8192]{2,1,0:T(8,128)(2,1)}, u32[]{:S(2)}) copy-start(bf16[1,128,8192]{2,1,0:T(8,128)(2,1)} %param.7) | copy-start | bytes 6291460
  7.2 202.0 %all-gather.3.cloned.1.call-start = ((), (), s32[]{:S(2)}) async-start(), calls=%async_computation.1 | async-start | bytes 2129920 | tf_op jit(solution)/shard_map/all_gather | solution.py:322
  7.9 398.4 %all-reduce.2.cloned.1.call-start = ((), (), s32[]{:S(2)}) async-start(), calls=%async_computation | async-start | bytes 8912896 | tf_op jit(solution)/shard_map/psum | solution.py:330
  8.7 0.8 copy-start.3
  9.5 0.9 copy-start.4
  10.4 0.9 copy-start.5
  205.1 1.3 copy-start.1
  206.5 2.8 copy-start.6
  216.3 0.7 copy-start.7
  406.3 4.3 %copy-start.2 = (bf16[128,8192]{1,0:T(8,128)(2,1)S(1)}, bf16[128,8192]{1,0:T(8,128)(2,1)}, u32[]{:S(2)}) copy-start(bf16[128,8192]{1,0:T(8,128)(2,1)} %copy-done.1) | copy-start | bytes 6291460
Sparse Core Ops, SparseCore 0:
  10.8 83.3 all-gather.2
  216.4 189.7 all-reduce.1

commit v2 on v1

--- a/solution.py
+++ b/solution.py
@@ -1,5 +1,3 @@
-import functools
-
 import jax
 import jax.numpy as jnp
 from jax import lax
@@ -14,6 +12,7 @@
 TR = 128
 RANK = 16
 WA = KV + TR
+WIDE = 1024 + 128
 ROWS = 128
 SUB = ROWS // NY
 COLS = NZ * NX * SUB
@@ -316,21 +315,195 @@
     )(g0, fz, aa, bb, ids)
 
 
+def reduce_kernel(
+    x_ref, vb_ref, low_ref, pick_ref,
+    oa_ref, ob_ref,
+    xv, gs, gm, gp, hop_l, hop_r, from_l, from_r, hs, js, zr, tall, fs, fin,
+    x_sem, p_s, p_r, x_s, x_r, z_s, z_r, t_s, t_r, f_s, f_r,
+):
+    y = lax.axis_index("section")
+    d = lax.axis_index("dp")
+    z = d // (NX * NC)
+    x = (d // NC) % NX
+    c = d % NC
+    sib = 1 - c
+    bf = jnp.bfloat16
+
+    def dev(zz, xx, cc):
+        return (y, zz * (NX * NC) + xx * NC + cc)
+
+    pending = []
+
+    def send(src, dst, ssem, rsem, device):
+        copy = pltpu.make_async_remote_copy(
+            src_ref=src, dst_ref=dst, send_sem=ssem, recv_sem=rsem,
+            device_id=device, device_id_type=MESH,
+        )
+        copy.start()
+        pending.append(copy)
+
+    def landed(dst, rsem):
+        pltpu.make_async_copy(dst, dst, rsem).wait()
+
+    load = pltpu.make_async_copy(x_ref, xv, x_sem)
+    load.start()
+    row = [
+        (dx, dc, (x + dx) % NX, (c + dc) % NC)
+        for dx in range(NX) for dc in range(NC) if dx or dc
+    ]
+    barrier = pltpu.get_barrier_semaphore()
+    for _, _, xx, cc in row:
+        pl.semaphore_signal(barrier, inc=1, device_id=dev(z, xx, cc), device_id_type=MESH)
+    for dz in range(1, NZ):
+        pl.semaphore_signal(barrier, inc=1, device_id=dev((z + dz) % NZ, x, c), device_id_type=MESH)
+    pl.semaphore_wait(barrier, 14)
+
+    eye = (
+        lax.broadcasted_iota(jnp.int32, (ROWS, ROWS), 0) == lax.broadcasted_iota(jnp.int32, (ROWS, ROWS), 1)
+    ).astype(bf)
+    back_t = mm_t(eye, vb_ref[:, KV:WA]).astype(bf)
+    low_t = mm_t(eye, low_ref[...]).astype(bf)
+    offsets = (2, 1, 3, 0)
+    load.wait()
+
+    def term(cc, i, ref):
+        xx = (x + offsets[i]) % NX
+        cols = pl.ds(pl.multiple_of((cc * NX + xx) * 1024, 1024), 1024)
+        ref[i, :, 0:1024] = mm(back_t, xv[:, cols]).astype(bf)
+        mine = vb_ref[:, pl.ds(pl.multiple_of(xx * 128, 128), 128)]
+        ref[i, :, 1024:WIDE] = (2.0 * mm(low_t, mine)).astype(bf)
+
+    for i in range(NX):
+        term(sib, i, gs)
+        send(gs.at[i], gp.at[i], p_s.at[i], p_r.at[i], dev(z, x, sib))
+    for i in range(NX):
+        term(c, i, gm)
+
+    h = ROWS // 2
+    top, bot = pl.ds(0, h), pl.ds(h, h)
+    xr, xl = (x + 1) % NX, (x + 3) % NX
+
+    def pair(i, rows):
+        return gm[i, rows, :].astype(jnp.float32) + gp[i, rows, :].astype(jnp.float32)
+
+    landed(gp.at[0], p_r.at[0])
+    hs[0] = pair(0, pl.ds(0, ROWS)).astype(bf)
+    send(hs.at[0, top], hop_l, x_s.at[0], x_r.at[0], dev(z, xr, c))
+    send(hs.at[0, bot], hop_r, x_s.at[1], x_r.at[1], dev(z, xl, c))
+    landed(gp.at[1], p_r.at[1])
+    hs[1, bot, :] = pair(1, bot).astype(bf)
+    send(hs.at[1, bot], from_l.at[bot], x_s.at[2], x_r.at[2], dev(z, xr, c))
+    landed(gp.at[2], p_r.at[2])
+    hs[2, top, :] = pair(2, top).astype(bf)
+    send(hs.at[2, top], from_r.at[top], x_s.at[3], x_r.at[3], dev(z, xl, c))
+    landed(hop_l, x_r.at[0])
+    hs[1, top, :] = (pair(1, top) + hop_l[...].astype(jnp.float32)).astype(bf)
+    send(hs.at[1, top], from_l.at[top], x_s.at[4], x_r.at[4], dev(z, xr, c))
+    landed(hop_r, x_r.at[1])
+    hs[2, bot, :] = (pair(2, bot) + hop_r[...].astype(jnp.float32)).astype(bf)
+    send(hs.at[2, bot], from_r.at[bot], x_s.at[5], x_r.at[5], dev(z, xl, c))
+    landed(gp.at[3], p_r.at[3])
+    landed(from_l.at[bot], x_r.at[2])
+    landed(from_r.at[top], x_r.at[3])
+    landed(from_l.at[top], x_r.at[4])
+    landed(from_r.at[bot], x_r.at[5])
+    for k in range(NZ):
+        rows = pl.ds(k * RANK, RANK)
+        total = pair(3, rows) + from_l[rows, :].astype(jnp.float32) + from_r[rows, :].astype(jnp.float32)
+        js[k] = total.astype(bf)
+    for dz in range(1, NZ):
+        to = (z + dz) % NZ
+        send(js.at[to], zr.at[dz], z_s.at[dz], z_r.at[dz], dev(to, x, c))
+    total = js[z].astype(jnp.float32)
+    for dz in range(1, NZ):
+        landed(zr.at[dz], z_r.at[dz])
+        total = total + zr[dz].astype(jnp.float32)
+    tall[z] = total.astype(bf)
+    for dz in range(1, NZ):
+        to = (z + dz) % NZ
+        send(tall.at[z], tall.at[z], t_s.at[dz], t_r.at[dz], dev(to, x, c))
+    for dz in range(1, NZ):
+        there = (z + NZ - dz) % NZ
+        landed(tall.at[there], t_r.at[dz])
+    fs[...] = mm(pick_ref[...], tall[...].reshape(TR, WIDE)).astype(bf).reshape(NC * NX, RANK, WIDE)
+    me = c * NX + x
+    for dx, dc, xx, cc in row:
+        j = dx * NC + dc
+        send(fs.at[cc * NX + xx], fin.at[me], f_s.at[j], f_r.at[j], dev(z, xx, cc))
+    fin[me] = fs[me]
+    for dx, dc, _, _ in row:
+        j = dx * NC + dc
+        there = ((c - dc + NC) % NC) * NX + (x - dx + NX) % NX
+        landed(fin.at[there], f_r.at[j])
+    for b in range(NC * NX):
+        oa_ref[:, b * 1024:(b + 1) * 1024] = fin[b, :, 0:1024].astype(jnp.float32)
+    for xx in range(NX):
+        ob_ref[:, xx * 128:(xx + 1) * 128] = fin[xx, :, 1024:WIDE].astype(jnp.float32)
+    for copy in pending:
+        copy.wait_send()
+
+
+def reduce_to_owners(inputs, vb, low, pick):
+    vmem = pl.BlockSpec(memory_space=pltpu.VMEM)
+    dma = pltpu.SemaphoreType.DMA
+    bf = jnp.bfloat16
+    return pl.pallas_call(
+        reduce_kernel,
+        out_shape=(
+            jax.ShapeDtypeStruct((RANK, D), jnp.float32),
+            jax.ShapeDtypeStruct((RANK, KV), jnp.float32),
+        ),
+        in_specs=[pl.BlockSpec(memory_space=pl.ANY), vmem, vmem, vmem],
+        out_specs=(vmem, vmem),
+        scratch_shapes=[
+            pltpu.VMEM((ROWS, D), bf),
+            pltpu.VMEM((NX, ROWS, WIDE), bf),
+            pltpu.VMEM((NX, ROWS, WIDE), bf),
+            pltpu.VMEM((NX, ROWS, WIDE), bf),
+            pltpu.VMEM((ROWS // 2, WIDE), bf),
+            pltpu.VMEM((ROWS // 2, WIDE), bf),
+            pltpu.VMEM((ROWS, WIDE), bf),
+            pltpu.VMEM((ROWS, WIDE), bf),
+            pltpu.VMEM((NX, ROWS, WIDE), bf),
+            pltpu.VMEM((NZ, RANK, WIDE), bf),
+            pltpu.VMEM((NZ, RANK, WIDE), bf),
+            pltpu.VMEM((NZ, RANK, WIDE), bf),
+            pltpu.VMEM((NC * NX, RANK, WIDE), bf),
+            pltpu.VMEM((NC * NX, RANK, WIDE), bf),
+            dma,
+            dma((NX,)),
+            dma((NX,)),
+            dma((6,)),
+            dma((6,)),
+            dma((NZ,)),
+            dma((NZ,)),
+            dma((NZ,)),
+            dma((NZ,)),
+            dma((NX * NC,)),
+            dma((NX * NC,)),
+        ],
+        compiler_params=pltpu.CompilerParams(
+            collective_id=1, has_side_effects=True, vmem_limit_bytes=40 * 2**20
+        ),
+        cost_estimate=pl.CostEstimate(flops=4 * 10**8, bytes_accessed=4 * 10**6, transcendentals=0),
+    )(inputs, vb, low, pick)
+
+
 def body(layer_inputs, top_grad, tenant_ids, owner_map, frozen, adapt_a, adapt_b):
     my_data = lax.axis_index("dp")
     inputs = layer_inputs[0]
     down = lax.all_gather(adapt_a[0], "dp", axis=0, tiled=True)
     grads, vb = chain(top_grad, frozen[0], adapt_a[0], adapt_b[0], tenant_ids[:, None])
-    values, back2 = vb[:, :KV], vb[:, KV:]
     columns = lax.broadcasted_iota(jnp.int32, (1, TR), 1) // RANK
     mask = (columns == tenant_ids[:, None]).astype(jnp.float32)
     low = (mask * mm(inputs, down)).astype(jnp.bfloat16)
-    sum_a = lax.dot_general(back2, inputs, (((0,), (0,)), ((), ())), preferred_element_type=jnp.float32)
-    sum_b = 2.0 * lax.dot_general(low, values, (((0,), (0,)), ((), ())), preferred_element_type=jnp.float32)
-    full = lax.psum(jnp.concatenate([sum_a, sum_b], axis=1), "dp")
-    owned = (owner_map == my_data).astype(jnp.float32)
-    mine = jnp.sum(full.reshape(-1, RANK, D + KV) * owned[:, None, None], axis=0)
-    return grads[None], mine[None, None, :, :D], mine[None, None, :, D:]
+    place = lax.broadcasted_iota(jnp.int32, (TR, TR), 0)
+    entry = lax.broadcasted_iota(jnp.int32, (TR, TR), 1)
+    block = place // RANK
+    target = (my_data // (NX * NC)) * (NX * NC) + (block % NX) * NC + block // NX
+    chosen = (jnp.repeat(owner_map, RANK)[None, :] == target) & (place % RANK == entry % RANK)
+    owned_a, owned_b = reduce_to_owners(inputs, vb, low, chosen.astype(jnp.bfloat16))
+    return grads[None], owned_a[None, None], owned_b[None, None]
 
 
 def solution(mesh):

time: 420 us -> 260 us (0.62)
  waiting for transfers between devices: 190 us -> 0.7 us
  Pallas kernels: 194 us -> 234 us
  other arithmetic: 7.48 us -> 0.19 us
    psum x1 -> x0, waiting for transfers between devices: 189 us -> none  [body(): full = lax.psum(jnp.concatenate([sum_a, sum_b], axis=1), 'dp')]
    pallas_call x0 -> x1, Pallas kernels: none -> 40.5 us  [reduce_to_owners(): pl.pallas_call(reduce_kernel, out_shape=(jax.ShapeDtypeStruct((RANK, D),...]
    concatenate x1 -> x0, other arithmetic: 4.6 us -> none  [body(): full = lax.psum(jnp.concatenate([sum_a, sum_b], axis=1), 'dp')]
  transfers between devices with their start and end apart: 2 -> 1, of which waited for: 1 -> 0; matrix products, arithmetic and copies ran while one was open for 1% -> 0% of each run, Pallas kernels for 46% -> 75%
where the time goes in v2:
time: 260 us; the launch traced here: 259 us
  Pallas kernels  234 us (90%)
  between operations  14.1 us (5%)
  local copies, waits for them, and re-layouts  7.58 us (3%)
    pallas_call x1, Pallas kernels, chain(): pl.pallas_call(chain_kernel, out_shape=(jax.ShapeDtypeStruct((ROWS, D), b...  194 us
    pallas_call x1, Pallas kernels, reduce_to_owners(): pl.pallas_call(reduce_kernel, out_shape=(jax.ShapeDtypeStruct((RANK, D),...  40.5 us
    unnamed x19, local copies, waits for them, and re-layouts  6.67 us
  transfers between devices with their start and end apart: 1, of which 0 were waited for; matrix products, arithmetic and copies ran while one was open for 0% of the time, Pallas kernels for 75%

profile of v2, /device:TPU:1, one launch (start us, length us, event | category | flops | bytes accessed | tf_op | source)
XLA Modules:
  0.0 259.2 jit_solution(3452492030806002959)
XLA Ops:
  7.2 0.0 all-gather.3.cloned.1.call-start
  7.2 0.7 all-gather.3.cloned.1.call-update
  7.9 0.8 copy.10.ids_ref
  8.7 0.0 copy-start.3
  8.7 0.8 copy-done.3
  9.4 0.9 copy-done.4
  10.4 0.9 copy-done.5
  11.3 193.8 %shard_map.94 = (bf16[128,8192]{1,0:T(8,128)(2,1)S(1)}, bf16[128,640]{1,0:T(8,128)(2,1)S(1)}) custom-call(bf16[128,8192]{1,0:T(8,128)(2,1)} %g0_ref.1, bf16[128,1024]{1,0:T(8,128)(2,1)S(1)} %bitcast.22, bf16[128,128]{1,0:T(8,128)(2,1)S(1)} %bitcast.20, bf16[128,512]{1,0:T(8,128)(2,1)S(1)} %bitcast.23, s32[128,1]{1,0:T(8,128)S(1)} %copy.10.ids_ref), custom_call_target="tpu_custom_call" | custom-call | flops 4000000000 | bytes 10000000 | tf_op jit(solution)/shard_map/pallas_call | solution.py:276
  205.1 0.0 copy-start.1
  205.1 1.3 copy-done.1
  206.4 0.0 copy-done.7
  206.4 0.1 broadcast_in_dim.18
  206.5 0.1 eq.33
  206.6 0.2 fusion.17.pick_ref
  206.8 0.0 all-gather.3.cloned.1.call-done
  206.8 0.0 copy-done
  206.8 0.0 copy-done.6
  206.8 2.3 fusion.5.low_ref
  209.1 0.0 copy-start.2
  209.1 40.5 %shard_map.95 = (f32[16,8192]{1,0:T(8,128)S(1)}, f32[16,512]{1,0:T(8,128)S(1)}) custom-call(bf16[128,8192]{1,0:T(8,128)(2,1)S(1)} %bitcast.17, bf16[128,640]{1,0:T(8,128)(2,1)S(1)} %get-tuple-element.8.vb_ref, bf16[128,128]{1,0:T(8,128)(2,1)S(1)} %fusion.5.low_ref, bf16[128,128]{1,0:T(8,128)(2,1)S(1)} %fusion.17.pick_ref), custom_call_target="tpu_custom_call" | custom-call | flops 400000000 | bytes 4000000 | tf_op jit(solution)/shard_map/pallas_call | solution.py:450
  249.7 0.0 copy-done.2
  249.7 1.3 copy.14
  251.0 0.8 copy.15
  251.8 0.6 copy.16
  (9 shorter events, 0.0 us)
Async XLA Ops:
  7.2 199.6 %all-gather.3.cloned.1.call-start = ((), (), s32[]{:S(2)}) async-start(), calls=%async_computation | async-start | bytes 2129920 | tf_op jit(solution)/shard_map/all_gather | solution.py:495
  8.7 0.8 copy-start.3
  9.4 0.9 copy-start.4
  10.4 0.9 copy-start.5
  11.3 195.1 %copy-start.7 = (s32[8]{0:T(128)S(1)}, s32[8]{0:T(128)}, u32[]{:S(2)}) copy-start(s32[8]{0:T(128)} %param.10) | copy-start | bytes 100
  11.3 195.5 %copy-start = (bf16[1,128,8192]{2,1,0:T(8,128)(2,1)S(1)}, bf16[1,128,8192]{2,1,0:T(8,128)(2,1)}, u32[]{:S(2)}) copy-start(bf16[1,128,8192]{2,1,0:T(8,128)(2,1)} %param.7) | copy-start | bytes 6291460
  11.3 195.5 %copy-start.6 = (s32[128]{0:T(128)S(1)}, s32[128]{0:T(128)}, u32[]{:S(2)}) copy-start(s32[128]{0:T(128)} %param.9) | copy-start | bytes 1540
  205.1 1.3 copy-start.1
  209.1 40.5 %copy-start.2 = (bf16[128,8192]{1,0:T(8,128)(2,1)S(1)}, bf16[128,8192]{1,0:T(8,128)(2,1)}, u32[]{:S(2)}) copy-start(bf16[128,8192]{1,0:T(8,128)(2,1)} %copy-done.1) | copy-start | bytes 6291460
Sparse Core Ops, SparseCore 0:
  10.8 83.5 all-gather.2

commit v3 on v1

v3 whole, which is shorter than its diff:
```python
import jax
import jax.numpy as jnp
from jax import lax
from jax.experimental import pallas as pl
from jax.experimental.pallas import tpu as pltpu
from jax.sharding import PartitionSpec as P

MESH = pl.DeviceIdType.MESH
NY, NZ, NX, NC = 4, 8, 4, 2
D = 8192
KV = 512
TR = 128
RANK = 16
WA = KV + TR
WIDE = 1024 + 128
STAGES = 5
PIECES = (("O", 3), ("W", 3), ("O", 2), ("W", 2), ("O", 1), ("W", 1), ("O", 0), ("A", 0), ("W", 0))
ROWS = 128
SUB = ROWS // NY
COLS = NZ * NX * SUB


def mm(a, b):
    return lax.dot_general(a, b, (((1,), (0,)), ((), ())), preferred_element_type=jnp.float32)


def mm_t(a, b):
    return lax.dot_general(a, b, (((1,), (1,)), ((), ())), preferred_element_type=jnp.float32)


def fused_kernel(
    g0_ref, x_ref, fz_ref, aa_ref, bb_ref, ids_ref, pick_ref,
    out_ref, oa_ref, ob_ref,
    ob, wab, afull, gall, rbuf, g0v, xv, gsend, pb, rsr, vball, bbuf, perm,
    gs, gm, gp, hop_l, hop_r, from_l, from_r, hs, js, zr, tall, fs, fin,
    ring_s, ring_r, y_s, yo_r, yw_r, b_r, load_sem, sib_sem, rs_s, rs_r, vb_s, vb_r, out_s, out_r, af_sem,
    p_s, p_r, x_s, x_r, z_s, z_r, t_s, t_r, f_s, f_r,
):
    y = lax.axis_index("section")
    d = lax.axis_index("dp")
    z = d // (NX * NC)
    x = (d // NC) % NX
    c = d % NC
    bf = jnp.bfloat16

    def dev(yy, zz, xx, cc):
        return (yy, zz * (NX * NC) + xx * NC + cc)

    xr, xl, xo = (x + 1) % NX, (x + NX - 1) % NX, (x + 2) % NX
    zr_, zl_ = (z + 1) % NZ, (z + NZ - 1) % NZ
    sib = 1 - c
    own = pl.ds(pl.multiple_of(c * ROWS, ROWS), ROWS)
    others = pl.ds(pl.multiple_of(sib * ROWS, ROWS), ROWS)
    pending = []

    def send(src, dst, ssem, rsem, device):
        copy = pltpu.make_async_remote_copy(
            src_ref=src, dst_ref=dst, send_sem=ssem, recv_sem=rsem,
            device_id=device, device_id_type=MESH,
        )
        copy.start()
        pending.append(copy)

    def landed(dst, rsem):
        pltpu.make_async_copy(dst, dst, rsem).wait()

    load = pltpu.make_async_copy(g0_ref, g0v, load_sem.at[0])
    load.start()
    load_x = pltpu.make_async_copy(x_ref, xv, load_sem.at[1])
    load_x.start()

    column = [
        (dq, dc, (y + dq) % NY, (c + dc) % NC)
        for dq in range(NY) for dc in range(NC) if dq or dc
    ]
    row = [
        (dx, dc, (x + dx) % NX, (c + dc) % NC)
        for dx in range(NX) for dc in range(NC) if dx or dc
    ]
    barrier = pltpu.get_barrier_semaphore()
    for _, _, yy, cc in column:
        pl.semaphore_signal(barrier, inc=1, device_id=dev(yy, z, x, cc), device_id_type=MESH)
    for dx, _, xx, cc in row:
        if dx:
            pl.semaphore_signal(barrier, inc=1, device_id=dev(y, z, xx, cc), device_id_type=MESH)
    for dz in range(1, NZ):
        pl.semaphore_signal(barrier, inc=1, device_id=dev(y, (z + dz) % NZ, x, c), device_id_type=MESH)
    pl.semaphore_wait(barrier, 20)

    for dq in range(NY):
        yy = (y + dq) % NY
        rows = pl.ds(pl.multiple_of(yy * SUB, SUB), SUB)
        parts = (
            (fz_ref.at[rows, pl.ds(KV, KV)], ob.at[y, z, x], yo_r.at[y]),
            (fz_ref.at[rows, pl.ds(0, KV)], wab.at[y, z, x, :, pl.ds(0, KV)], yw_r.at[y]),
            (aa_ref.at[rows, :], wab.at[y, z, x, :, pl.ds(KV, TR)], yw_r.at[y]),
            (bb_ref, bbuf.at[y], b_r.at[y]),
        )
        for i, (src, dst, rsem) in enumerate(parts):
            if dq:
                send(src, dst, y_s.at[dq, i], rsem, dev(yy, z, x, c))
            else:
                pltpu.make_async_copy(src, dst, rsem).start()
    pltpu.make_async_copy(aa_ref, afull.at[z, x, c], load_sem.at[2]).start()

    half = SUB // 2

    def ring(piece, k):
        name, s = PIECES[piece]

        def zb(by):
            return (z + by + NZ) % NZ

        if name == "A":
            quarter = ROWS // 4
            top, low = (0, 2 * quarter), (2 * quarter, 2 * quarter)
            low_lo, low_hi = (2 * quarter, quarter), (3 * quarter, quarter)

            def at(zz, xx, rows):
                return afull.at[zz, xx, c, pl.ds(*rows)]

            lo, hi = at(zb(-3), x, low_lo), at(zb(3), x, low_hi)
            far_lo, far_hi = at(zb(4), x, low_lo), at(zb(4), x, low_hi)
        else:
            buf, width = (ob, KV) if name == "O" else (wab, WA)
            top, low = (0, half), (half, half)

            def at(zz, xx, rows):
                return buf.at[s, zz, xx, pl.ds(*rows)]

            def lanes(zz, first, count):
                return buf.at[s, zz, x, pl.ds(*low), pl.ds(first, count)]

            lo, hi = lanes(zb(-3), 0, 256), lanes(zb(3), 256, width - 256)
            far_lo, far_hi = lanes(zb(4), 0, 256), lanes(zb(4), 256, width - 256)

        everything = slice(None)
        first, last = pl.ds(0, 2), pl.ds(2, 2)
        to_x = [(z, xr), (z, xl), (z, xo)]
        up, down = (zr_, x), (zl_, x)
        a_recv = [
            (at(z, xl, top), at(z, xr, top), at(z, xo, top)),
            (at(zb(-1), everything, top), at(zb(1), everything, top)),
            (at(zb(-2), everything, top), at(zb(2), everything, top)),
            (at(zb(-3), everything, top), at(zb(3), everything, top)),
            (at(zb(4), first, top), at(zb(4), last, top)),
        ]
        a_send = [
            [(at(z, x, top), to) for to in to_x],
            [(at(z, everything, top), up), (at(z, everything, top), down)],
            [(at(zb(-1), everything, top), up), (at(zb(1), everything, top), down)],
            [(at(zb(-2), everything, top), up), (at(zb(2), everything, top), down)],
            [(at(zb(-3), first, top), up), (at(zb(3), last, top), down)],
        ]
        b_recv = [
            (at(zb(-1), x, low), at(zb(1), x, low)),
            (at(zb(-2), x, low), at(zb(2), x, low)),
            (at(zb(-3), x, low), at(zb(3), x, low)),
            (far_lo, far_hi),
            (at(everything, xl, low), at(everything, xr, low), at(everything, xo, low)),
        ]
        b_send = [
            [(at(z, x, low), up), (at(z, x, low), down)],
            [(at(zb(-1), x, low), up), (at(zb(1), x, low), down)],
            [(at(zb(-2), x, low), up), (at(zb(2), x, low), down)],
            [(lo, up), (hi, down)],
            [(at(everything, x, low), to) for to in to_x],
        ]
        if k == 0:
            if name == "A":
                landed(afull.at[z, x, c], load_sem.at[2])
            else:
                landed(buf.at[s, z, x], (yo_r if name == "O" else yw_r).at[s])
        else:
            for part, recv in enumerate((a_recv, b_recv)):
                for way, ref in enumerate(recv[k - 1]):
                    landed(ref, ring_r.at[piece, part, k - 1, way])
        if k < STAGES:
            for part, moves in enumerate((a_send, b_send)):
                for way, (src, (zz, xx)) in enumerate(moves[k]):
                    send(src, src, ring_s.at[piece, part, k, way], ring_r.at[piece, part, k, way],
                         dev(y, zz, xx, c))

    def compact():
        load.wait()
        source = lax.broadcasted_iota(jnp.int32, (NX * NC * ROWS, ROWS), 0)
        target = lax.broadcasted_iota(jnp.int32, (NX * NC * ROWS, ROWS), 1)
        base = (target // SUB) * (NC * ROWS) + target % SUB + y * SUB
        mine = (source == base + c * ROWS).astype(jnp.bfloat16)
        other = (source == base + sib * ROWS).astype(jnp.bfloat16)

        for zz in range(NZ):
            block = g0v[:, zz * 1024:(zz + 1) * 1024]
            gsend[:, zz * ROWS:(zz + 1) * ROWS] = mm(block, other).astype(jnp.bfloat16)
        send(gsend, gall.at[NY, own], sib_sem.at[0], sib_sem.at[1], dev(y, z, x, sib))
        for zz in range(NZ):
            block = g0v[:, zz * 1024:(zz + 1) * 1024]
            gall[NY, own, zz * ROWS:(zz + 1) * ROWS] = mm(block, mine).astype(jnp.bfloat16)
        landed(gsend, sib_sem.at[1])

        p_in = lax.broadcasted_iota(jnp.int32, (NY * ROWS, NY * ROWS), 0)
        p_out = lax.broadcasted_iota(jnp.int32, (NY * ROWS, NY * ROWS), 1)
        want = ((p_out // SUB) % NY) * ROWS + (p_out // ROWS) * SUB + p_out % SUB
        perm[...] = (p_in == want).astype(jnp.bfloat16)

    def block_of(yy, cc):
        return pl.ds(pl.multiple_of(cc * ROWS + yy * SUB, SUB), SUB)

    def partial(s):
        right = ob[s].reshape(COLS, KV)
        pb[s] = mm(gall[s + 1], right).astype(jnp.bfloat16)
        for dq, dc, yy, cc in column:
            j = dq * NC + dc
            send(pb.at[s, block_of(yy, cc)], rsr.at[s, j], rs_s.at[s, j], rs_r.at[s, j], dev(yy, z, x, cc))

    def finalise(s):
        total = pb[s, block_of(y, c), :].astype(jnp.float32)
        for dq, dc, _, _ in column:
            j = dq * NC + dc
            landed(rsr.at[s, j], rs_r.at[s, j])
            total = total + rsr[s, j].astype(jnp.float32)
        value = total.astype(jnp.bfloat16)
        landed(bbuf.at[s], b_r.at[s])
        ids = ids_ref[pl.ds(pl.multiple_of(y * SUB, SUB), SUB), :]
        columns = lax.broadcasted_iota(jnp.int32, (SUB, TR), 1) // RANK
        mask = (columns == ids).astype(jnp.float32)
        back = (mask * mm_t(value, bbuf[s])).astype(jnp.bfloat16)
        here = block_of(y, c)
        vball[s, here, 0:KV] = value
        vball[s, here, KV:WA] = (2.0 * back.astype(jnp.float32)).astype(jnp.bfloat16)
        for dq, dc, yy, cc in column:
            j = dq * NC + dc
            send(vball.at[s, here], vball.at[s, here], vb_s.at[s, j], vb_r.at[s, j], dev(yy, z, x, cc))

    def arrive_vb(s):
        for dq, dc, _, _ in column:
            j = dq * NC + dc
            there = block_of((y - dq + NY) % NY, (c - dc + NC) % NC)
            landed(vball.at[s, there], vb_r.at[s, j])

    def update(s):
        if s:
            arrive_vb(s)
        for i in range(4):
            cols = slice(i * 256, (i + 1) * 256)
            right = wab[s, 2 * i:2 * i + 2].reshape(256, WA)
            delta = mm_t(vball[s], right)
            gall[s, :, cols] = (gall[s + 1, :, cols].astype(jnp.float32) + delta).astype(jnp.bfloat16)

    def deliver(s):
        dq = (s - y + NY) % NY
        send(gall.at[s, others], rbuf.at[y, c], out_s.at[s, 1], out_r.at[dq * 2 + 1], dev(s, z, x, sib))
        direct = pltpu.make_async_remote_copy(
            src_ref=gall.at[s, own], dst_ref=rbuf.at[y, c], send_sem=out_s.at[s, 0], recv_sem=out_r.at[dq * 2],
            device_id=dev(s, z, x, c), device_id_type=MESH,
        )
        keep = pltpu.make_async_copy(gall.at[s, own], rbuf.at[y, c], out_r.at[0])

        @pl.when(y != s)
        def _():
            direct.start()

        @pl.when(y == s)
        def _():
            keep.start()

    def low_terms():
        load_x.wait()
        landed(afull.at[:, :, sib], af_sem.at[1])
        columns = lax.broadcasted_iota(jnp.int32, (ROWS, TR), 1) // RANK
        mask = (columns == ids_ref[...]).astype(jnp.float32)
        total = jnp.zeros((ROWS, TR), jnp.float32)
        for k in range(4):
            right = afull[2 * k:2 * k + 2].reshape(2048, TR)
            total = total + mm(xv[:, k * 2048:(k + 1) * 2048], right)
        low = (mask * total).astype(bf)
        return mm_t(eye, low).astype(bf)

    offsets = (2, 1, 3, 0)

    def term(cc, i, ref):
        xx = (x + offsets[i]) % NX
        cols = pl.ds(pl.multiple_of((cc * NX + xx) * 1024, 1024), 1024)
        ref[i, :, 0:1024] = mm(back_t, xv[:, cols]).astype(bf)
        mine = vball[y, own, pl.ds(pl.multiple_of(xx * 128, 128), 128)]
        ref[i, :, 1024:WIDE] = (2.0 * mm(low_t, mine)).astype(bf)

    eye = (
        lax.broadcasted_iota(jnp.int32, (ROWS, ROWS), 0) == lax.broadcasted_iota(jnp.int32, (ROWS, ROWS), 1)
    ).astype(bf)

    compact()
    for t in range(13):
        for piece in range(9):
            k = t - max(0, piece - 1)
            if 0 <= k <= STAGES:
                ring(piece, k)
        if t >= 5 and t % 2 == 1:
            i = (t - 5) // 2
            if i > 0:
                update(NY - i)
            partial(NY - 1 - i)
            if t == 11:
                send(afull.at[:, :, c], afull.at[:, :, c], af_sem.at[0], af_sem.at[1], dev(y, z, x, sib))
        elif t >= 6:
            finalise(NY - 1 - (t - 6) // 2)
    for s in (3, 2, 1):
        deliver(s)
    low_t = low_terms()
    arrive_vb(0)
    back_t = mm_t(eye, vball[y, own, KV:WA]).astype(bf)

    for i in range(NX):
        term(sib, i, gs)
        send(gs.at[i], gp.at[i], p_s.at[i], p_r.at[i], dev(y, z, x, sib))
    for i in range(NX):
        term(c, i, gm)
    update(0)
    deliver(0)

    h = ROWS // 2
    top, bot = pl.ds(0, h), pl.ds(h, h)

    def pair(i, rows):
        return gm[i, rows, :].astype(jnp.float32) + gp[i, rows, :].astype(jnp.float32)

    landed(gp.at[0], p_r.at[0])
    hs[0] = pair(0, pl.ds(0, ROWS)).astype(bf)
    send(hs.at[0, top], hop_l, x_s.at[0], x_r.at[0], dev(y, z, xr, c))
    send(hs.at[0, bot], hop_r, x_s.at[1], x_r.at[1], dev(y, z, xl, c))
    landed(gp.at[1], p_r.at[1])
    hs[1, bot, :] = pair(1, bot).astype(bf)
    send(hs.at[1, bot], from_l.at[bot], x_s.at[2], x_r.at[2], dev(y, z, xr, c))
    landed(gp.at[2], p_r.at[2])
    hs[2, top, :] = pair(2, top).astype(bf)
    send(hs.at[2, top], from_r.at[top], x_s.at[3], x_r.at[3], dev(y, z, xl, c))
    landed(hop_l, x_r.at[0])
    hs[1, top, :] = (pair(1, top) + hop_l[...].astype(jnp.float32)).astype(bf)
    send(hs.at[1, top], from_l.at[top], x_s.at[4], x_r.at[4], dev(y, z, xr, c))
    landed(hop_r, x_r.at[1])
    hs[2, bot, :] = (pair(2, bot) + hop_r[...].astype(jnp.float32)).astype(bf)
    send(hs.at[2, bot], from_r.at[bot], x_s.at[5], x_r.at[5], dev(y, z, xl, c))
    landed(gp.at[3], p_r.at[3])
    landed(from_l.at[bot], x_r.at[2])
    landed(from_r.at[top], x_r.at[3])
    landed(from_l.at[top], x_r.at[4])
    landed(from_r.at[bot], x_r.at[5])
    for k in range(NZ):
        rows = pl.ds(k * RANK, RANK)
        total = pair(3, rows) + from_l[rows, :].astype(jnp.float32) + from_r[rows, :].astype(jnp.float32)
        js[k] = total.astype(bf)
    for dz in range(1, NZ):
        to = (z + dz) % NZ
        send(js.at[to], zr.at[dz], z_s.at[dz], z_r.at[dz], dev(y, to, x, c))
    total = js[z].astype(jnp.float32)
    for dz in range(1, NZ):
        landed(zr.at[dz], z_r.at[dz])
        total = total + zr[dz].astype(jnp.float32)
    tall[z] = total.astype(bf)
    for dz in range(1, NZ):
        to = (z + dz) % NZ
        send(tall.at[z], tall.at[z], t_s.at[dz], t_r.at[dz], dev(y, to, x, c))
    for j in range(NY * NC):
        landed(rbuf.at[(y - j // 2 + NY) % NY, (c - j % 2 + NC) % NC], out_r.at[j])
    for zz in range(NZ):
        for cc in range(NC):
            block = jnp.concatenate([rbuf[q, cc, :, zz * ROWS:(zz + 1) * ROWS] for q in range(NY)], axis=1)
            mixed = mm(block, perm[...]).astype(jnp.bfloat16)
            for xx in range(NX):
                at = zz * 1024 + xx * 256 + cc * ROWS
                out_ref[:, at:at + ROWS] = mixed[:, xx * ROWS:(xx + 1) * ROWS]

    for dz in range(1, NZ):
        there = (z + NZ - dz) % NZ
        landed(tall.at[there], t_r.at[dz])
    fs[...] = mm(pick_ref[...], tall[...].reshape(TR, WIDE)).astype(bf).reshape(NC * NX, RANK, WIDE)
    me = c * NX + x
    for dx, dc, xx, cc in row:
        j = dx * NC + dc
        send(fs.at[cc * NX + xx], fin.at[me], f_s.at[j], f_r.at[j], dev(y, z, xx, cc))
    fin[me] = fs[me]
    for dx, dc, _, _ in row:
        j = dx * NC + dc
        there = ((c - dc + NC) % NC) * NX + (x - dx + NX) % NX
        landed(fin.at[there], f_r.at[j])
    for b in range(NC * NX):
        oa_ref[:, b * 1024:(b + 1) * 1024] = fin[b, :, 0:1024].astype(jnp.float32)
    for xx in range(NX):
        ob_ref[:, xx * 128:(xx + 1) * 128] = fin[xx, :, 1024:WIDE].astype(jnp.float32)
    for s in range(NY):
        @pl.when(y != s)
        def _(s=s):
            pltpu.make_async_copy(gall.at[s, own], gall.at[s, own], out_s.at[s, 0]).wait()
    for copy in pending:
        copy.wait_send()


def fused(g0, inputs, fz, aa, bb, ids, pick):
    vmem = pl.BlockSpec(memory_space=pltpu.VMEM)
    anywhere = pl.BlockSpec(memory_space=pl.ANY)
    dma = pltpu.SemaphoreType.DMA
    bf = jnp.bfloat16
    return pl.pallas_call(
        fused_kernel,
        out_shape=(
            jax.ShapeDtypeStruct((ROWS, D), bf),
            jax.ShapeDtypeStruct((RANK, D), jnp.float32),
            jax.ShapeDtypeStruct((RANK, KV), jnp.float32),
        ),
        in_specs=[anywhere] * 5 + [vmem] * 2,
        out_specs=(vmem, vmem, vmem),
        scratch_shapes=[
            pltpu.VMEM((NY, NZ, NX, SUB, KV), bf),
            pltpu.VMEM((NY, NZ, NX, SUB, WA), bf),
            pltpu.VMEM((NZ, NX, NC, ROWS, TR), bf),
            pltpu.VMEM((NY + 1, NC * ROWS, COLS), bf),
            pltpu.VMEM((NY, NC, ROWS, COLS), bf),
            pltpu.VMEM((ROWS, D), bf),
            pltpu.VMEM((ROWS, D), bf),
            pltpu.VMEM((ROWS, COLS), bf),
            pltpu.VMEM((NY, NC * ROWS, KV), bf),
            pltpu.VMEM((NY, NY * NC, SUB, KV), bf),
            pltpu.VMEM((NY, NC * ROWS, WA), bf),
            pltpu.VMEM((NY, TR, KV), bf),
            pltpu.VMEM((NY * ROWS, NY * ROWS), bf),
            pltpu.VMEM((NX, ROWS, WIDE), bf),
            pltpu.VMEM((NX, ROWS, WIDE), bf),
            pltpu.VMEM((NX, ROWS, WIDE), bf),
            pltpu.VMEM((ROWS // 2, WIDE), bf),
            pltpu.VMEM((ROWS // 2, WIDE), bf),
            pltpu.VMEM((ROWS, WIDE), bf),
            pltpu.VMEM((ROWS, WIDE), bf),
            pltpu.VMEM((NX, ROWS, WIDE), bf),
            pltpu.VMEM((NZ, RANK, WIDE), bf),
            pltpu.VMEM((NZ, RANK, WIDE), bf),
            pltpu.VMEM((NZ, RANK, WIDE), bf),
            pltpu.VMEM((NC * NX, RANK, WIDE), bf),
            pltpu.VMEM((NC * NX, RANK, WIDE), bf),
            dma((9, 2, STAGES, 3)),
            dma((9, 2, STAGES, 3)),
            dma((NY, 4)),
            dma((NY,)),
            dma((NY,)),
            dma((NY,)),
            dma((3,)),
            dma((2,)),
            dma((NY, NY * NC)),
            dma((NY, NY * NC)),
            dma((NY, NY * NC)),
            dma((NY, NY * NC)),
            dma((NY, 2)),
            dma((NY * NC,)),
            dma((2,)),
            dma((NX,)),
            dma((NX,)),
            dma((6,)),
            dma((6,)),
            dma((NZ,)),
            dma((NZ,)),
            dma((NZ,)),
            dma((NZ,)),
            dma((NX * NC,)),
            dma((NX * NC,)),
        ],
        compiler_params=pltpu.CompilerParams(
            collective_id=0, has_side_effects=True, vmem_limit_bytes=56 * 2**20
        ),
        cost_estimate=pl.CostEstimate(flops=5 * 10**9, bytes_accessed=10**7, transcendentals=0),
    )(g0, inputs, fz, aa, bb, ids, pick)


def body(layer_inputs, top_grad, tenant_ids, owner_map, frozen, adapt_a, adapt_b):
    my_data = lax.axis_index("dp")
    place = lax.broadcasted_iota(jnp.int32, (TR, TR), 0)
    entry = lax.broadcasted_iota(jnp.int32, (TR, TR), 1)
    block = place // RANK
    target = (my_data // (NX * NC)) * (NX * NC) + (block % NX) * NC + block // NX
    chosen = (jnp.repeat(owner_map, RANK)[None, :] == target) & (place % RANK == entry % RANK)
    grads, owned_a, owned_b = fused(
        top_grad, layer_inputs[0], frozen[0], adapt_a[0], adapt_b[0],
        tenant_ids[:, None], chosen.astype(jnp.bfloat16),
    )
    return grads[None], owned_a[None, None], owned_b[None, None]


def solution(mesh):
    return jax.shard_map(
        body,
        mesh=mesh,
        in_specs=(
            P("section", "dp", None),
            P("dp", None),
            P("dp"),
            P(),
            P("section", "dp", None),
            P("section", "dp", None),
            P("section", None, None),
        ),
        out_specs=(
            P("section", "dp", None),
            P("section", "dp", None, None),
            P("section", "dp", None, None),
        ),
        check_vma=False,
    )
```

time: 420 us -> 176 us (0.42)
  the two profiles are of different devices: /device:TPU:1 before, /device:TPU:25 now
where the time goes in v3:
time: 176 us
  Pallas kernels  168 us (95%)
  local copies, waits for them, and re-layouts  6.76 us (4%)
    pallas_call x1, Pallas kernels, fused(): pl.pallas_call(fused_kernel, out_shape=(jax.ShapeDtypeStruct((ROWS, D), b...  168 us
    unnamed x7, local copies, waits for them, and re-layouts  4.57 us

profile of v3, /device:TPU:25, one launch (start us, length us, event | category | flops | bytes accessed | tf_op | source)
XLA Modules:
  0.0 176.0 jit_solution(624964966439317452)
XLA Ops:
  0.7 0.7 broadcast_in_dim.16
  1.4 0.1 eq.17
  1.5 0.8 fusion.9.pick_ref
  2.3 1.4 copy.10.ids_ref
  3.7 167.7 %shard_map.94 = (bf16[128,8192]{1,0:T(8,128)(2,1)}, f32[16,8192]{1,0:T(8,128)}, f32[16,512]{1,0:T(8,128)}) custom-call(bf16[128,8192]{1,0:T(8,128)(2,1)} %g0_ref.1, bf16[128,8192]{1,0:T(8,128)(2,1)} %bitcast.12, bf16[128,1024]{1,0:T(8,128)(2,1)} %bitcast.13, bf16[128,128]{1,0:T(8,128)(2,1)} %bitcast.15, bf16[128,512]{1,0:T(8,128)(2,1)} %bitcast.14, ...), custom_call_target="tpu_custom_call" | custom-call | flops 5000000000 | bytes 10000000 | tf_op jit(solution)/shard_map/pallas_call | solution.py:403
  171.4 0.0 copy-start
  171.4 0.0 copy-start.1
  171.4 3.2 %copy.14 = bf16[1,128,8192]{2,1,0:T(8,128)(2,1)} copy(bf16[1,128,8192]{2,1,0:T(8,128)(2,1)} %bitcast.8) | data formatting | bytes 4194304
  174.6 0.0 copy-done
  174.6 0.8 copy.15
  175.4 0.0 copy-done.1
  175.4 0.6 copy.16
  (3 shorter events, 0.0 us)
Async XLA Ops:
  171.4 3.2 %copy-start = (f32[16,8192]{1,0:T(8,128)S(1)}, f32[16,8192]{1,0:T(8,128)}, u32[]{:S(2)}) copy-start(f32[16,8192]{1,0:T(8,128)} %get-tuple-element.7) | copy-start | bytes 1572868
  171.4 4.0 %copy-start.1 = (f32[16,512]{1,0:T(8,128)S(1)}, f32[16,512]{1,0:T(8,128)}, u32[]{:S(2)}) copy-start(f32[16,512]{1,0:T(8,128)} %get-tuple-element.8) | copy-start | bytes 98308

commit v4 on v3

--- a/solution.py
+++ b/solution.py
@@ -15,6 +15,7 @@
 WIDE = 1024 + 128
 STAGES = 5
 PIECES = (("O", 3), ("W", 3), ("O", 2), ("W", 2), ("O", 1), ("W", 1), ("O", 0), ("A", 0), ("W", 0))
+DONE = {piece: i for i, piece in enumerate(PIECES)}
 ROWS = 128
 SUB = ROWS // NY
 COLS = NZ * NX * SUB
@@ -29,12 +30,12 @@
 
 
 def fused_kernel(
-    g0_ref, x_ref, fz_ref, aa_ref, bb_ref, ids_ref, pick_ref,
+    g0_ref, x_ref, fz_ref, aa_ref, bb_ref, ids_ref, owner_ref,
     out_ref, oa_ref, ob_ref,
-    ob, wab, afull, gall, rbuf, g0v, xv, gsend, pb, rsr, vball, bbuf, perm,
+    ob, wab, afull, gall, rbuf, g0v, xv, gsend, pb, rsr, vball, bbuf, perm, mask, pick, outv,
     gs, gm, gp, hop_l, hop_r, from_l, from_r, hs, js, zr, tall, fs, fin,
     ring_s, ring_r, y_s, yo_r, yw_r, b_r, load_sem, sib_sem, rs_s, rs_r, vb_s, vb_r, out_s, out_r, af_sem,
-    p_s, p_r, x_s, x_r, z_s, z_r, t_s, t_r, f_s, f_r,
+    p_s, p_r, x_s, x_r, z_s, z_r, t_s, t_r, f_s, f_r, o_sem,
 ):
     y = lax.axis_index("section")
     d = lax.axis_index("dp")
@@ -94,7 +95,6 @@
             (fz_ref.at[rows, pl.ds(KV, KV)], ob.at[y, z, x], yo_r.at[y]),
             (fz_ref.at[rows, pl.ds(0, KV)], wab.at[y, z, x, :, pl.ds(0, KV)], yw_r.at[y]),
             (aa_ref.at[rows, :], wab.at[y, z, x, :, pl.ds(KV, TR)], yw_r.at[y]),
-            (bb_ref, bbuf.at[y], b_r.at[y]),
         )
         for i, (src, dst, rsem) in enumerate(parts):
             if dq:
@@ -102,6 +102,25 @@
             else:
                 pltpu.make_async_copy(src, dst, rsem).start()
     pltpu.make_async_copy(aa_ref, afull.at[z, x, c], load_sem.at[2]).start()
+
+    def send_b():
+        for dq in range(1, NY):
+            send(bb_ref, bbuf.at[y], y_s.at[dq, 3], b_r.at[y], dev((y + dq) % NY, z, x, c))
+        pltpu.make_async_copy(bb_ref, bbuf.at[y], b_r.at[y]).start()
+
+    eye = lax.broadcasted_iota(jnp.int32, (ROWS, ROWS), 0) == lax.broadcasted_iota(jnp.int32, (ROWS, ROWS), 1)
+    tenant = jnp.sum(eye.astype(jnp.float32) * ids_ref[...].astype(jnp.float32), axis=1, keepdims=True)
+    slot = lax.broadcasted_iota(jnp.int32, (ROWS, TR), 1) // RANK
+    mask[...] = (slot.astype(jnp.float32) == tenant).astype(jnp.float32)
+    eye = eye.astype(bf)
+    owner = jnp.zeros((TR, TR), jnp.int32)
+    for k in range(TR // RANK):
+        owner = owner + (slot == k).astype(jnp.int32) * owner_ref[k]
+    place = lax.broadcasted_iota(jnp.int32, (TR, TR), 0)
+    entry = lax.broadcasted_iota(jnp.int32, (TR, TR), 1)
+    block = place // RANK
+    target = z * (NX * NC) + (block % NX) * NC + block // NX
+    pick[...] = ((owner == target) & (place % RANK == entry % RANK)).astype(bf)
 
     half = SUB // 2
 
@@ -221,10 +240,8 @@
             total = total + rsr[s, j].astype(jnp.float32)
         value = total.astype(jnp.bfloat16)
         landed(bbuf.at[s], b_r.at[s])
-        ids = ids_ref[pl.ds(pl.multiple_of(y * SUB, SUB), SUB), :]
-        columns = lax.broadcasted_iota(jnp.int32, (SUB, TR), 1) // RANK
-        mask = (columns == ids).astype(jnp.float32)
-        back = (mask * mm_t(value, bbuf[s])).astype(jnp.bfloat16)
+        here_mask = mask[pl.ds(pl.multiple_of(y * SUB, SUB), SUB), :]
+        back = (here_mask * mm_t(value, bbuf[s])).astype(jnp.bfloat16)
         here = block_of(y, c)
         vball[s, here, 0:KV] = value
         vball[s, here, KV:WA] = (2.0 * back.astype(jnp.float32)).astype(jnp.bfloat16)
@@ -267,13 +284,11 @@
     def low_terms():
         load_x.wait()
         landed(afull.at[:, :, sib], af_sem.at[1])
-        columns = lax.broadcasted_iota(jnp.int32, (ROWS, TR), 1) // RANK
-        mask = (columns == ids_ref[...]).astype(jnp.float32)
         total = jnp.zeros((ROWS, TR), jnp.float32)
         for k in range(4):
             right = afull[2 * k:2 * k + 2].reshape(2048, TR)
             total = total + mm(xv[:, k * 2048:(k + 1) * 2048], right)
-        low = (mask * total).astype(bf)
+        low = (mask[...] * total).astype(bf)
         return mm_t(eye, low).astype(bf)
 
     offsets = (2, 1, 3, 0)
@@ -285,25 +300,27 @@
         mine = vball[y, own, pl.ds(pl.multiple_of(xx * 128, 128), 128)]
         ref[i, :, 1024:WIDE] = (2.0 * mm(low_t, mine)).astype(bf)
 
-    eye = (
-        lax.broadcasted_iota(jnp.int32, (ROWS, ROWS), 0) == lax.broadcasted_iota(jnp.int32, (ROWS, ROWS), 1)
-    ).astype(bf)
-
-    compact()
-    for t in range(13):
+    for t in range(12):
         for piece in range(9):
             k = t - max(0, piece - 1)
-            if 0 <= k <= STAGES:
+            if 0 <= k < STAGES:
                 ring(piece, k)
+        if t == 0:
+            compact()
+        if t == 1:
+            send_b()
         if t >= 5 and t % 2 == 1:
             i = (t - 5) // 2
             if i > 0:
+                ring(DONE["W", NY - i], STAGES)
                 update(NY - i)
+            ring(DONE["O", NY - 1 - i], STAGES)
             partial(NY - 1 - i)
-            if t == 11:
-                send(afull.at[:, :, c], afull.at[:, :, c], af_sem.at[0], af_sem.at[1], dev(y, z, x, sib))
         elif t >= 6:
             finalise(NY - 1 - (t - 6) // 2)
+    ring(DONE["A", 0], STAGES)
+    send(afull.at[:, :, c], afull.at[:, :, c], af_sem.at[0], af_sem.at[1], dev(y, z, x, sib))
+    finalise(0)
     for s in (3, 2, 1):
         deliver(s)
     low_t = low_terms()
@@ -315,8 +332,6 @@
         send(gs.at[i], gp.at[i], p_s.at[i], p_r.at[i], dev(y, z, x, sib))
     for i in range(NX):
         term(c, i, gm)
-    update(0)
-    deliver(0)
 
     h = ROWS // 2
     top, bot = pl.ds(0, h), pl.ds(h, h)
@@ -334,6 +349,9 @@
     landed(gp.at[2], p_r.at[2])
     hs[2, top, :] = pair(2, top).astype(bf)
     send(hs.at[2, top], from_r.at[top], x_s.at[3], x_r.at[3], dev(y, z, xl, c))
+    ring(DONE["W", 0], STAGES)
+    update(0)
+    deliver(0)
     landed(hop_l, x_r.at[0])
     hs[1, top, :] = (pair(1, top) + hop_l[...].astype(jnp.float32)).astype(bf)
     send(hs.at[1, top], from_l.at[top], x_s.at[4], x_r.at[4], dev(y, z, xr, c))
@@ -368,12 +386,14 @@
             mixed = mm(block, perm[...]).astype(jnp.bfloat16)
             for xx in range(NX):
                 at = zz * 1024 + xx * 256 + cc * ROWS
-                out_ref[:, at:at + ROWS] = mixed[:, xx * ROWS:(xx + 1) * ROWS]
+                outv[:, at:at + ROWS] = mixed[:, xx * ROWS:(xx + 1) * ROWS]
+        cols = pl.ds(zz * 1024, 1024)
+        pltpu.make_async_copy(outv.at[:, cols], out_ref.at[:, cols], o_sem.at[zz]).start()
 
     for dz in range(1, NZ):
         there = (z + NZ - dz) % NZ
         landed(tall.at[there], t_r.at[dz])
-    fs[...] = mm(pick_ref[...], tall[...].reshape(TR, WIDE)).astype(bf).reshape(NC * NX, RANK, WIDE)
+    fs[...] = mm(pick[...], tall[...].reshape(TR, WIDE)).astype(bf).reshape(NC * NX, RANK, WIDE)
     me = c * NX + x
     for dx, dc, xx, cc in row:
         j = dx * NC + dc
@@ -391,11 +411,14 @@
         @pl.when(y != s)
         def _(s=s):
             pltpu.make_async_copy(gall.at[s, own], gall.at[s, own], out_s.at[s, 0]).wait()
+    for zz in range(NZ):
+        cols = pl.ds(zz * 1024, 1024)
+        pltpu.make_async_copy(outv.at[:, cols], out_ref.at[:, cols], o_sem.at[zz]).wait()
     for copy in pending:
         copy.wait_send()
 
 
-def fused(g0, inputs, fz, aa, bb, ids, pick):
+def fused(g0, inputs, fz, aa, bb, ids, owner):
     vmem = pl.BlockSpec(memory_space=pltpu.VMEM)
     anywhere = pl.BlockSpec(memory_space=pl.ANY)
     dma = pltpu.SemaphoreType.DMA
@@ -407,8 +430,8 @@
             jax.ShapeDtypeStruct((RANK, D), jnp.float32),
             jax.ShapeDtypeStruct((RANK, KV), jnp.float32),
         ),
-        in_specs=[anywhere] * 5 + [vmem] * 2,
-        out_specs=(vmem, vmem, vmem),
+        in_specs=[anywhere] * 5 + [vmem, pl.BlockSpec(memory_space=pltpu.SMEM)],
+        out_specs=(anywhere, vmem, vmem),
         scratch_shapes=[
             pltpu.VMEM((NY, NZ, NX, SUB, KV), bf),
             pltpu.VMEM((NY, NZ, NX, SUB, WA), bf),
@@ -423,6 +446,9 @@
             pltpu.VMEM((NY, NC * ROWS, WA), bf),
             pltpu.VMEM((NY, TR, KV), bf),
             pltpu.VMEM((NY * ROWS, NY * ROWS), bf),
+            pltpu.VMEM((ROWS, TR), jnp.float32),
+            pltpu.VMEM((TR, TR), bf),
+            pltpu.VMEM((ROWS, D), bf),
             pltpu.VMEM((NX, ROWS, WIDE), bf),
             pltpu.VMEM((NX, ROWS, WIDE), bf),
             pltpu.VMEM((NX, ROWS, WIDE), bf),
@@ -461,24 +487,18 @@
             dma((NZ,)),
             dma((NX * NC,)),
             dma((NX * NC,)),
+            dma((NZ,)),
         ],
         compiler_params=pltpu.CompilerParams(
             collective_id=0, has_side_effects=True, vmem_limit_bytes=56 * 2**20
         ),
         cost_estimate=pl.CostEstimate(flops=5 * 10**9, bytes_accessed=10**7, transcendentals=0),
-    )(g0, inputs, fz, aa, bb, ids, pick)
+    )(g0, inputs, fz, aa, bb, ids, owner)
 
 
 def body(layer_inputs, top_grad, tenant_ids, owner_map, frozen, adapt_a, adapt_b):
-    my_data = lax.axis_index("dp")
-    place = lax.broadcasted_iota(jnp.int32, (TR, TR), 0)
-    entry = lax.broadcasted_iota(jnp.int32, (TR, TR), 1)
-    block = place // RANK
-    target = (my_data // (NX * NC)) * (NX * NC) + (block % NX) * NC + block // NX
-    chosen = (jnp.repeat(owner_map, RANK)[None, :] == target) & (place % RANK == entry % RANK)
     grads, owned_a, owned_b = fused(
-        top_grad, layer_inputs[0], frozen[0], adapt_a[0], adapt_b[0],
-        tenant_ids[:, None], chosen.astype(jnp.bfloat16),
+        top_grad, layer_inputs[0], frozen[0], adapt_a[0], adapt_b[0], tenant_ids[None, :], owner_map
     )
     return grads[None], owned_a[None, None], owned_b[None, None]
 

time: 176 us -> 153 us (0.87)
  the two profiles are of different devices: /device:TPU:25 before, /device:TPU:1 now
where the time goes in v4:
time: 153 us; the launch traced here: 152 us
  Pallas kernels  147 us (96%)
  local copies, waits for them, and re-layouts  4.57 us (3%)
    pallas_call x1, Pallas kernels, fused(): pl.pallas_call(fused_kernel, out_shape=(jax.ShapeDtypeStruct((ROWS, D), b...  147 us
    unnamed x7, local copies, waits for them, and re-layouts  4.57 us

profile of v4, /device:TPU:1, one launch (start us, length us, event | category | flops | bytes accessed | tf_op | source)
XLA Modules:
  0.0 152.4 jit_solution(1250041506757695460)
XLA Ops:
  0.6 147.2 %shard_map.94 = (bf16[128,8192]{1,0:T(8,128)(2,1)}, f32[16,8192]{1,0:T(8,128)}, f32[16,512]{1,0:T(8,128)}) custom-call(bf16[128,8192]{1,0:T(8,128)(2,1)} %g0_ref.1, bf16[128,8192]{1,0:T(8,128)(2,1)} %bitcast.11, bf16[128,1024]{1,0:T(8,128)(2,1)} %bitcast.12, bf16[128,128]{1,0:T(8,128)(2,1)} %bitcast.14, bf16[128,512]{1,0:T(8,128)(2,1)} %bitcast.13, ...), custom_call_target="tpu_custom_call" | custom-call | flops 5000000000 | bytes 10000000 | tf_op jit(solution)/shard_map/pallas_call | solution.py:426
  147.9 0.0 copy-start
  147.9 0.0 copy-start.1
  147.9 3.2 %copy.13 = bf16[1,128,8192]{2,1,0:T(8,128)(2,1)} copy(bf16[1,128,8192]{2,1,0:T(8,128)(2,1)} %bitcast.8) | data formatting | bytes 4194304
  151.0 0.0 copy-done
  151.0 0.8 copy.14
  151.8 0.0 copy-done.1
  151.8 0.6 copy.15
Async XLA Ops:
  147.9 3.2 %copy-start = (f32[16,8192]{1,0:T(8,128)S(1)}, f32[16,8192]{1,0:T(8,128)}, u32[]{:S(2)}) copy-start(f32[16,8192]{1,0:T(8,128)} %get-tuple-element.7) | copy-start | bytes 1572868
  147.9 4.0 %copy-start.1 = (f32[16,512]{1,0:T(8,128)S(1)}, f32[16,512]{1,0:T(8,128)}, u32[]{:S(2)}) copy-start(f32[16,512]{1,0:T(8,128)} %get-tuple-element.8) | copy-start | bytes 98308

commit v5 on v4

--- a/solution.py
+++ b/solution.py
@@ -335,49 +335,66 @@
 
     h = ROWS // 2
     top, bot = pl.ds(0, h), pl.ds(h, h)
-
-    def pair(i, rows):
-        return gm[i, rows, :].astype(jnp.float32) + gp[i, rows, :].astype(jnp.float32)
+    parts = (pl.ds(0, 640), pl.ds(640, 512))
+
+    def pair(i, rows, cut):
+        return gm[i, rows, cut].astype(jnp.float32) + gp[i, rows, cut].astype(jnp.float32)
 
     landed(gp.at[0], p_r.at[0])
-    hs[0] = pair(0, pl.ds(0, ROWS)).astype(bf)
-    send(hs.at[0, top], hop_l, x_s.at[0], x_r.at[0], dev(y, z, xr, c))
-    send(hs.at[0, bot], hop_r, x_s.at[1], x_r.at[1], dev(y, z, xl, c))
+    for n, cut in enumerate(parts):
+        hs[0, :, cut] = pair(0, pl.ds(0, ROWS), cut).astype(bf)
+        send(hs.at[0, top, cut], hop_l.at[:, cut], x_s.at[n, 0], x_r.at[n, 0], dev(y, z, xr, c))
+        send(hs.at[0, bot, cut], hop_r.at[:, cut], x_s.at[n, 1], x_r.at[n, 1], dev(y, z, xl, c))
     landed(gp.at[1], p_r.at[1])
-    hs[1, bot, :] = pair(1, bot).astype(bf)
-    send(hs.at[1, bot], from_l.at[bot], x_s.at[2], x_r.at[2], dev(y, z, xr, c))
     landed(gp.at[2], p_r.at[2])
-    hs[2, top, :] = pair(2, top).astype(bf)
-    send(hs.at[2, top], from_r.at[top], x_s.at[3], x_r.at[3], dev(y, z, xl, c))
+    for n, cut in enumerate(parts):
+        hs[1, bot, cut] = pair(1, bot, cut).astype(bf)
+        send(hs.at[1, bot, cut], from_l.at[bot, cut], x_s.at[n, 2], x_r.at[n, 2], dev(y, z, xr, c))
+        hs[2, top, cut] = pair(2, top, cut).astype(bf)
+        send(hs.at[2, top, cut], from_r.at[top, cut], x_s.at[n, 3], x_r.at[n, 3], dev(y, z, xl, c))
     ring(DONE["W", 0], STAGES)
     update(0)
     deliver(0)
-    landed(hop_l, x_r.at[0])
-    hs[1, top, :] = (pair(1, top) + hop_l[...].astype(jnp.float32)).astype(bf)
-    send(hs.at[1, top], from_l.at[top], x_s.at[4], x_r.at[4], dev(y, z, xr, c))
-    landed(hop_r, x_r.at[1])
-    hs[2, bot, :] = (pair(2, bot) + hop_r[...].astype(jnp.float32)).astype(bf)
-    send(hs.at[2, bot], from_r.at[bot], x_s.at[5], x_r.at[5], dev(y, z, xl, c))
+    for n, cut in enumerate(parts):
+        landed(hop_l.at[:, cut], x_r.at[n, 0])
+        hs[1, top, cut] = (pair(1, top, cut) + hop_l[:, cut].astype(jnp.float32)).astype(bf)
+        send(hs.at[1, top, cut], from_l.at[top, cut], x_s.at[n, 4], x_r.at[n, 4], dev(y, z, xr, c))
+        landed(hop_r.at[:, cut], x_r.at[n, 1])
+        hs[2, bot, cut] = (pair(2, bot, cut) + hop_r[:, cut].astype(jnp.float32)).astype(bf)
+        send(hs.at[2, bot, cut], from_r.at[bot, cut], x_s.at[n, 5], x_r.at[n, 5], dev(y, z, xl, c))
     landed(gp.at[3], p_r.at[3])
-    landed(from_l.at[bot], x_r.at[2])
-    landed(from_r.at[top], x_r.at[3])
-    landed(from_l.at[top], x_r.at[4])
-    landed(from_r.at[bot], x_r.at[5])
-    for k in range(NZ):
-        rows = pl.ds(k * RANK, RANK)
-        total = pair(3, rows) + from_l[rows, :].astype(jnp.float32) + from_r[rows, :].astype(jnp.float32)
-        js[k] = total.astype(bf)
-    for dz in range(1, NZ):
-        to = (z + dz) % NZ
-        send(js.at[to], zr.at[dz], z_s.at[dz], z_r.at[dz], dev(y, to, x, c))
-    total = js[z].astype(jnp.float32)
-    for dz in range(1, NZ):
-        landed(zr.at[dz], z_r.at[dz])
-        total = total + zr[dz].astype(jnp.float32)
-    tall[z] = total.astype(bf)
-    for dz in range(1, NZ):
-        to = (z + dz) % NZ
-        send(tall.at[z], tall.at[z], t_s.at[dz], t_r.at[dz], dev(y, to, x, c))
+    for n, cut in enumerate(parts):
+        landed(from_l.at[bot, cut], x_r.at[n, 2])
+        landed(from_r.at[top, cut], x_r.at[n, 3])
+        landed(from_l.at[top, cut], x_r.at[n, 4])
+        landed(from_r.at[bot, cut], x_r.at[n, 5])
+        for k in range(NZ):
+            rows = pl.ds(k * RANK, RANK)
+            total = pair(3, rows, cut) + from_l[rows, cut].astype(jnp.float32) + from_r[rows, cut].astype(jnp.float32)
+            js[k, :, cut] = total.astype(bf)
+        for dz in range(1, NZ):
+            to = (z + dz) % NZ
+            send(js.at[to, :, cut], zr.at[dz, :, cut], z_s.at[n, dz], z_r.at[n, dz], dev(y, to, x, c))
+    for n, cut in enumerate(parts):
+        total = js[z, :, cut].astype(jnp.float32)
+        for dz in range(1, NZ):
+            landed(zr.at[dz, :, cut], z_r.at[n, dz])
+            total = total + zr[dz, :, cut].astype(jnp.float32)
+        tall[z, :, cut] = total.astype(bf)
+        for dz in range(1, NZ):
+            to = (z + dz) % NZ
+            send(tall.at[z, :, cut], tall.at[z, :, cut], t_s.at[n, dz], t_r.at[n, dz], dev(y, to, x, c))
+    me = c * NX + x
+    for n, cut in enumerate(parts):
+        for dz in range(1, NZ):
+            there = (z + NZ - dz) % NZ
+            landed(tall.at[there, :, cut], t_r.at[n, dz])
+        gathered = tall[:, :, cut].reshape(TR, cut.size)
+        fs[:, :, cut] = mm(pick[...], gathered).astype(bf).reshape(NC * NX, RANK, cut.size)
+        for dx, dc, xx, cc in row:
+            j = dx * NC + dc
+            send(fs.at[cc * NX + xx, :, cut], fin.at[me, :, cut], f_s.at[n, j], f_r.at[n, j], dev(y, z, xx, cc))
+    fin[me] = fs[me]
     for j in range(NY * NC):
         landed(rbuf.at[(y - j // 2 + NY) % NY, (c - j % 2 + NC) % NC], out_r.at[j])
     for zz in range(NZ):
@@ -390,19 +407,11 @@
         cols = pl.ds(zz * 1024, 1024)
         pltpu.make_async_copy(outv.at[:, cols], out_ref.at[:, cols], o_sem.at[zz]).start()
 
-    for dz in range(1, NZ):
-        there = (z + NZ - dz) % NZ
-        landed(tall.at[there], t_r.at[dz])
-    fs[...] = mm(pick[...], tall[...].reshape(TR, WIDE)).astype(bf).reshape(NC * NX, RANK, WIDE)
-    me = c * NX + x
-    for dx, dc, xx, cc in row:
-        j = dx * NC + dc
-        send(fs.at[cc * NX + xx], fin.at[me], f_s.at[j], f_r.at[j], dev(y, z, xx, cc))
-    fin[me] = fs[me]
-    for dx, dc, _, _ in row:
-        j = dx * NC + dc
-        there = ((c - dc + NC) % NC) * NX + (x - dx + NX) % NX
-        landed(fin.at[there], f_r.at[j])
+    for n, cut in enumerate(parts):
+        for dx, dc, _, _ in row:
+            j = dx * NC + dc
+            there = ((c - dc + NC) % NC) * NX + (x - dx + NX) % NX
+            landed(fin.at[there, :, cut], f_r.at[n, j])
     for b in range(NC * NX):
         oa_ref[:, b * 1024:(b + 1) * 1024] = fin[b, :, 0:1024].astype(jnp.float32)
     for xx in range(NX):
@@ -479,14 +488,14 @@
             dma((2,)),
             dma((NX,)),
             dma((NX,)),
-            dma((6,)),
-            dma((6,)),
-            dma((NZ,)),
-            dma((NZ,)),
-            dma((NZ,)),
-            dma((NZ,)),
-            dma((NX * NC,)),
-            dma((NX * NC,)),
+            dma((2, 6)),
+            dma((2, 6)),
+            dma((2, NZ)),
+            dma((2, NZ)),
+            dma((2, NZ)),
+            dma((2, NZ)),
+            dma((2, NX * NC)),
+            dma((2, NX * NC)),
             dma((NZ,)),
         ],
         compiler_params=pltpu.CompilerParams(

time: 153 us -> 151 us (0.987)
    pallas_call x1, Pallas kernels: 147 us -> 146 us  [fused(): pl.pallas_call(fused_kernel, out_shape=(jax.ShapeDtypeStruct((ROWS, D), b...]
where the time goes in v5:
time: 151 us
  Pallas kernels  146 us (97%)
  local copies, waits for them, and re-layouts  4.57 us (3%)
    pallas_call x1, Pallas kernels, fused(): pl.pallas_call(fused_kernel, out_shape=(jax.ShapeDtypeStruct((ROWS, D), b...  146 us
    unnamed x7, local copies, waits for them, and re-layouts  4.57 us

profile of v5, /device:TPU:1, one launch (start us, length us, event | category | flops | bytes accessed | tf_op | source)
XLA Modules:
  0.0 150.8 jit_solution(12660879929975878442)
XLA Ops:
  0.6 145.6 %shard_map.94 = (bf16[128,8192]{1,0:T(8,128)(2,1)}, f32[16,8192]{1,0:T(8,128)}, f32[16,512]{1,0:T(8,128)}) custom-call(bf16[128,8192]{1,0:T(8,128)(2,1)} %g0_ref.1, bf16[128,8192]{1,0:T(8,128)(2,1)} %bitcast.11, bf16[128,1024]{1,0:T(8,128)(2,1)} %bitcast.12, bf16[128,128]{1,0:T(8,128)(2,1)} %bitcast.14, bf16[128,512]{1,0:T(8,128)(2,1)} %bitcast.13, ...), custom_call_target="tpu_custom_call" | custom-call | flops 5000000000 | bytes 10000000 | tf_op jit(solution)/shard_map/pallas_call | solution.py:435
  146.3 0.0 copy-start
  146.3 0.0 copy-start.1
  146.3 3.2 %copy.13 = bf16[1,128,8192]{2,1,0:T(8,128)(2,1)} copy(bf16[1,128,8192]{2,1,0:T(8,128)(2,1)} %bitcast.8) | data formatting | bytes 4194304
  149.4 0.0 copy-done
  149.4 0.8 copy.14
  150.2 0.0 copy-done.1
  150.2 0.6 copy.15
Async XLA Ops:
  146.3 3.2 %copy-start = (f32[16,8192]{1,0:T(8,128)S(1)}, f32[16,8192]{1,0:T(8,128)}, u32[]{:S(2)}) copy-start(f32[16,8192]{1,0:T(8,128)} %get-tuple-element.7) | copy-start | bytes 1572868
  146.3 4.0 %copy-start.1 = (f32[16,512]{1,0:T(8,128)S(1)}, f32[16,512]{1,0:T(8,128)}, u32[]{:S(2)}) copy-start(f32[16,512]{1,0:T(8,128)} %get-tuple-element.8) | copy-start | bytes 98308

commit v6 on v5

--- a/solution.py
+++ b/solution.py
@@ -88,15 +88,15 @@
         pl.semaphore_signal(barrier, inc=1, device_id=dev(y, (z + dz) % NZ, x, c), device_id_type=MESH)
     pl.semaphore_wait(barrier, 20)
 
-    for dq in range(NY):
-        yy = (y + dq) % NY
-        rows = pl.ds(pl.multiple_of(yy * SUB, SUB), SUB)
-        parts = (
-            (fz_ref.at[rows, pl.ds(KV, KV)], ob.at[y, z, x], yo_r.at[y]),
-            (fz_ref.at[rows, pl.ds(0, KV)], wab.at[y, z, x, :, pl.ds(0, KV)], yw_r.at[y]),
-            (aa_ref.at[rows, :], wab.at[y, z, x, :, pl.ds(KV, TR)], yw_r.at[y]),
-        )
-        for i, (src, dst, rsem) in enumerate(parts):
+    for i in range(3):
+        for dq in range(NY):
+            yy = (y + dq) % NY
+            rows = pl.ds(pl.multiple_of(yy * SUB, SUB), SUB)
+            src, dst, rsem = (
+                (fz_ref.at[rows, pl.ds(KV, KV)], ob.at[y, z, x], yo_r.at[y]),
+                (fz_ref.at[rows, pl.ds(0, KV)], wab.at[y, z, x, :, pl.ds(0, KV)], yw_r.at[y]),
+                (aa_ref.at[rows, :], wab.at[y, z, x, :, pl.ds(KV, TR)], yw_r.at[y]),
+            )[i]
             if dq:
                 send(src, dst, y_s.at[dq, i], rsem, dev(yy, z, x, c))
             else:

time: 151 us -> 151 us (level)
  no operation moved by 1% of the time
where the time goes in v6:
time: 151 us
  Pallas kernels  146 us (97%)
  local copies, waits for them, and re-layouts  4.57 us (3%)
    pallas_call x1, Pallas kernels, fused(): pl.pallas_call(fused_kernel, out_shape=(jax.ShapeDtypeStruct((ROWS, D), b...  146 us
    unnamed x7, local copies, waits for them, and re-layouts  4.57 us

profile of v6, /device:TPU:1, one launch (start us, length us, event | category | flops | bytes accessed | tf_op | source)
XLA Modules:
  0.0 151.1 jit_solution(17303656216784733140)
XLA Ops:
  0.6 145.9 %shard_map.94 = (bf16[128,8192]{1,0:T(8,128)(2,1)}, f32[16,8192]{1,0:T(8,128)}, f32[16,512]{1,0:T(8,128)}) custom-call(bf16[128,8192]{1,0:T(8,128)(2,1)} %g0_ref.1, bf16[128,8192]{1,0:T(8,128)(2,1)} %bitcast.11, bf16[128,1024]{1,0:T(8,128)(2,1)} %bitcast.12, bf16[128,128]{1,0:T(8,128)(2,1)} %bitcast.14, bf16[128,512]{1,0:T(8,128)(2,1)} %bitcast.13, ...), custom_call_target="tpu_custom_call" | custom-call | flops 5000000000 | bytes 10000000 | tf_op jit(solution)/shard_map/pallas_call | solution.py:435
  146.5 0.0 copy-start
  146.5 0.0 copy-start.1
  146.5 3.2 %copy.13 = bf16[1,128,8192]{2,1,0:T(8,128)(2,1)} copy(bf16[1,128,8192]{2,1,0:T(8,128)(2,1)} %bitcast.8) | data formatting | bytes 4194304
  149.7 0.0 copy-done
  149.7 0.8 copy.14
  150.5 0.0 copy-done.1
  150.5 0.6 copy.15
Async XLA Ops:
  146.5 3.2 %copy-start = (f32[16,8192]{1,0:T(8,128)S(1)}, f32[16,8192]{1,0:T(8,128)}, u32[]{:S(2)}) copy-start(f32[16,8192]{1,0:T(8,128)} %get-tuple-element.7) | copy-start | bytes 1572868
  146.5 4.0 %copy-start.1 = (f32[16,512]{1,0:T(8,128)S(1)}, f32[16,512]{1,0:T(8,128)}, u32[]{:S(2)}) copy-start(f32[16,512]{1,0:T(8,128)} %get-tuple-element.8) | copy-start | bytes 98308
